TPU v7x, 512 devices: a whole 4x4x16 slice. The times are simulated.
512 devices in a mesh: section: 32 (over x_hi, z), dp: 16 (over y, x_lo, core).
Axes of the slice: x: 4 (x_hi: 2, x_lo: 2; x = x_hi * 2 + x_lo), y: 4, z: 16, core: 2. Of those that a mesh axis runs over, the one named last changes fastest.
Arguments:
- stored_inputs: bfloat16 [32, 16, 33, 8, 8192], P('section', 'dp')
- slot_ids: int32 [32, 16, 33], P('section', 'dp'), may hold values from 0 to 32, as said below
- incoming: bfloat16 [32, 16, 8, 8192], P('section', 'dp'), may hold values from -6 to 6
- delta_exp: int32 [32, 16, 16, 8, 64], P('section', 'dp'), may hold values from -7 to -4
- grad_exp: int32 [32, 16, 15, 8, 64], P('section', 'dp'), may hold values from -7 to -4
- norm_gain: float32 [32, 8192], P('section'), may hold values from 0.5 to 1.5
- down_weight: bfloat16 [32, 8192, 64], P('section', 'dp'), may hold values from -0.0625 to 0.0625
- up_weight: bfloat16 [32, 64, 8192], P('section', None, 'dp'), may hold values from -0.09375 to 0.09375
Outputs:
- grad_down: bfloat16 [32, 8192, 64], P('section', 'dp')
- grad_up: bfloat16 [32, 64, 8192], P('section', None, 'dp')
- next_delta: bfloat16 [32, 16, 8, 8192], P('section', 'dp')
Inputs may be any that keep to these rules, and one draw needn't show every extreme that they name: Each row slot_ids[s, d, :] holds every slot number once.
All inputs are finite; a program needn't handle non-finite values.
Results may differ from a plain program's by a relative error of at most 0.025.
Values may be sent and summed in bfloat16 or wider, within the bound.
A program may use at most 64 MiB of HBM per device.

v0:
```python
import jax
import jax.numpy as jnp
from jax import lax
from jax.sharding import PartitionSpec as P

K = 16


EPSILON = 1e-05
LOWEST = -7
HIGHEST = -4


def passed_along(x, axis, by):
    devices = lax.axis_size(axis)
    pairs = [(i, i + by) for i in range(devices) if 0 <= i + by < devices]
    return lax.ppermute(x, axis, pairs)


def powers(exponent):
    running = jnp.zeros(exponent.shape, jnp.float32)
    for degree in range(LOWEST, HIGHEST + 1):
        running = running + jnp.where(
            exponent == degree, jnp.float32(2.0**degree), jnp.float32(0.0)
        )
    return running


def quantize(values, exponent):
    scales = powers(exponent)[..., None]
    blocked = values.reshape(values.shape[:-1] + (exponent.shape[-1], 128))
    levels = jnp.clip(blocked / scales, -127.0, 127.0).astype(jnp.bfloat16)
    levels = lax.optimization_barrier(levels)
    restored = levels.astype(jnp.float32) * scales
    return restored.reshape(values.shape).astype(jnp.bfloat16)


def norm_rows(inputs, gain_row):
    widened = inputs.astype(jnp.float32)
    inverse = lax.rsqrt(jnp.mean(widened * widened, axis=-1, keepdims=True) + EPSILON)
    normed = (widened * inverse * gain_row).astype(jnp.bfloat16)
    return (widened, inverse, normed)


def send_forward(sent_delta):
    return passed_along(sent_delta, "section", 1)


def send_backward(returned):
    return passed_along(returned, "section", -1)


def pick(table, tick):
    return lax.dynamic_index_in_dim(table, tick, 0, keepdims=False)


def join_rows(first, middle, final_rows):
    stacked = jnp.concatenate([first[None], middle, final_rows[None]], axis=0)
    return stacked.reshape(-1, first.shape[-1])


def per_device(
    stored_inputs, slot_ids, incoming, delta_exp, grad_exp, norm_gain, down_weight, up_weight
):
    memory = stored_inputs[0, 0]
    slot_order = slot_ids[0, 0]
    delta_table = delta_exp[0, 0]
    grad_table = grad_exp[0, 0]
    gain_row = norm_gain[0]
    down_full, up_full = (
        lax.all_gather(down_weight[0], "dp", axis=0, tiled=True),
        lax.all_gather(up_weight[0], "dp", axis=1, tiled=True),
    )
    is_last = lax.axis_index("section") == lax.axis_size("section") - 1
    rows_per = memory.shape[1]

    def take_slot(column):
        return lax.dynamic_index_in_dim(memory, slot_order[column], 0, keepdims=False)

    above = passed_along(jnp.take(memory, slot_order[1 : K + 1], axis=0), "section", -1)
    own_rows = jnp.take(memory, slot_order[0:K], axis=0)
    copy_table = jnp.where(is_last, own_rows, above)

    def copy_row(tick):
        return pick(copy_table, tick)

    def process(tick, inputs, arrived_grad, final):
        widened, inverse, normed = norm_rows(inputs, gain_row)
        back_inputs = jnp.where(is_last, inputs, take_slot(K + 1 + tick))
        back_widened, back_inverse, back_normed = norm_rows(back_inputs, gain_row)
        both = jnp.dot(
            jnp.concatenate([normed, back_normed], axis=0),
            down_full,
            preferred_element_type=jnp.float32,
        )
        before = both[:rows_per]
        back_before = both[rows_per:]
        hidden = jax.nn.silu(before).astype(jnp.bfloat16)
        output = widened + jnp.dot(hidden, up_full, preferred_element_type=jnp.float32)
        distance = output - copy_row(tick).astype(jnp.float32)
        sent_delta = quantize(distance, pick(delta_table, tick))
        back_hidden = jax.nn.silu(back_before).astype(jnp.bfloat16)
        cotangent = jnp.where(is_last, distance.astype(jnp.bfloat16), arrived_grad)
        slope_grad = lax.dot_general(
            cotangent, up_full, (((1,), (1,)), ((), ())), preferred_element_type=jnp.float32
        )
        gate_value = jax.nn.sigmoid(back_before)
        slope_grad = (slope_grad * gate_value * (1.0 + back_before * (1.0 - gate_value))).astype(
            jnp.bfloat16
        )
        returned = None
        if not final:
            through = (
                lax.dot_general(
                    slope_grad,
                    down_full,
                    (((1,), (1,)), ((), ())),
                    preferred_element_type=jnp.float32,
                )
                * gain_row
            )
            inner_mean = jnp.mean(through * back_widened, axis=-1, keepdims=True)
            result = (
                cotangent.astype(jnp.float32)
                + back_inverse * through
                - back_widened * back_inverse**3 * inner_mean
            )
            returned = quantize(result, pick(grad_table, tick))
        return (sent_delta, returned, (back_normed, slope_grad, back_hidden, cotangent))

    def advance(sent_delta, returned, tick, final):
        arrived = send_forward(sent_delta)
        inputs = (take_slot(tick).astype(jnp.float32) + arrived.astype(jnp.float32)).astype(
            jnp.bfloat16
        )
        arrived_grad = send_backward(returned)
        return process(tick, inputs, arrived_grad, final)

    sent_delta, returned, first_rows = process(0, take_slot(0), incoming[0, 0], False)

    def middle_tick(carry, tick):
        new_sent, new_returned, rows = advance(carry[0], carry[1], tick, False)
        return ((new_sent, new_returned), rows)

    carried, middle_rows = lax.scan(
        middle_tick, (sent_delta, returned), jnp.arange(1, K - 1, dtype=jnp.int32)
    )
    sent_delta, unused, final_rows = advance(carried[0], carried[1], K - 1, True)
    next_delta = sent_delta[None, None]
    normed_all = join_rows(first_rows[0], middle_rows[0], final_rows[0])
    slope_all = join_rows(first_rows[1], middle_rows[1], final_rows[1])
    hidden_all = join_rows(first_rows[2], middle_rows[2], final_rows[2])
    cotangent_all = join_rows(first_rows[3], middle_rows[3], final_rows[3])
    factor = 1.0 / (K * rows_per)
    down_term = lax.dot_general(
        normed_all, slope_all, (((0,), (0,)), ((), ())), preferred_element_type=jnp.float32
    )
    up_term = lax.dot_general(
        cotangent_all, hidden_all, (((0,), (0,)), ((), ())), preferred_element_type=jnp.float32
    )
    partial_value = jnp.concatenate([down_term, up_term], axis=1)
    summed = lax.psum_scatter(
        partial_value.astype(jnp.bfloat16), "dp", scatter_dimension=0, tiled=True
    ).astype(jnp.float32)
    width = down_term.shape[1]
    down_part = summed[:, :width]
    up_part = summed[:, width:].T
    grad_down = (down_part * factor).astype(jnp.bfloat16)[None]
    grad_up = (up_part * factor).astype(jnp.bfloat16)[None]
    return (grad_down, grad_up, next_delta)


def solution(mesh):
    return jax.shard_map(
        per_device,
        mesh=mesh,
        in_specs=(
            P("section", "dp", None, None, None),
            P("section", "dp", None),
            P("section", "dp", None, None),
            P("section", "dp", None, None, None),
            P("section", "dp", None, None, None),
            P("section", None),
            P("section", "dp", None),
            P("section", None, "dp"),
        ),
        out_specs=(
            P("section", "dp", None),
            P("section", None, "dp"),
            P("section", "dp", None, None),
        ),
        check_vma=False,
    )
```

profile of v0, /device:TPU:1, one launch (start us, length us, event | category | flops | bytes accessed | tf_op | source)
XLA Modules:
  0.0 644.3 jit_solution(7397021931175280072)
XLA Ops:
  9.7 2.9 gather_fusion.1
  27.5 2.9 gather_fusion
  32.9 25.2 %all-gather.5.cloned.1.call-done = bf16[1,8192,64]{2,1,0:T(8,128)(2,1)} async-done(((bf16[1,512,64]{2,1,0:T(8,128)(2,1)}), bf16[1,8192,64]{2,1,0:T(8,128)(2,1)}) %all-gather.5.cloned.1.call-update) | async-done | bytes 1048592 | tf_op jit(solution)/shard_map/all_gather | solution.py:71
  58.0 2.0 fusion.71
  60.0 3.3 select_select_fusion
  63.3 68.3 %all-gather.7.cloned.1.call-done = bf16[1,64,8192]{2,1,0:T(8,128)(2,1)} async-done(((bf16[1,64,512]{2,1,0:T(8,128)(2,1)}), bf16[1,64,8192]{2,1,0:T(8,128)(2,1)}) %all-gather.7.cloned.1.call-update) | async-done | bytes 1048592 | tf_op jit(solution)/shard_map/all_gather | solution.py:72
  137.7 369.8 %while.22 = (s32[]{:T(128)}, bf16[8,8192]{1,0:T(8,128)(2,1)}, bf16[8,8192]{1,0:T(8,128)(2,1)}, bf16[14,8,8192]{2,1,0:T(8,128)(2,1)}, bf16[14,8,64]{2,1,0:T(8,128...) while((s32[]{:T(128)}, bf16[8,8192]{1,0:T(8,128)(2,1)}, ...), condition=%wide.region_7.9_spmd, body=%wide.region_3.8_spmd.sunk | while | flops 45634096 | bytes 9738780 | solution.py:145
  137.7 3.2 collective-permute-start
  162.4 4.0 collective-permute-start
  188.0 4.0 collective-permute-start
  213.6 4.7 collective-permute-start
  239.8 5.2 collective-permute-start
  266.5 5.2 collective-permute-start
  293.3 5.2 collective-permute-start
  320.1 5.2 collective-permute-start
  346.9 5.2 collective-permute-start
  373.6 5.2 collective-permute-start
  400.4 5.2 collective-permute-start
  427.2 5.2 collective-permute-start
  453.9 5.2 collective-permute-start
  480.7 5.2 collective-permute-start
  507.5 5.3 collective-permute-start.3
  514.3 2.5 copy.17
  528.2 108.0 %reduce-scatter.2.cloned.1.call-done = bf16[512,128]{0,1:T(8,128)(2,1)} async-done(((bf16[8192,128]{0,1:T(8,128)(2,1)}), bf16[512,128]{0,1:T(8,128)(2,1)}) %reduce-scatter.2.cloned.1.call-update) | async-done | bytes 131088 | tf_op jit(solution)/shard_map/reduce_scatter | solution.py:162
  (385 shorter events, 202.6 us)
Async XLA Ops:
  7.2 50.9 %all-gather.5.cloned.1.call-start = ((), (), s32[]{:S(2)}) async-start(), calls=%async_computation.2 | async-start | bytes 2228224 | tf_op jit(solution)/shard_map/all_gather | solution.py:71
  8.8 122.7 %all-gather.7.cloned.1.call-start = ((), (), s32[]{:S(2)}) async-start(), calls=%async_computation.3 | async-start | bytes 1114112 | tf_op jit(solution)/shard_map/all_gather | solution.py:72
  14.3 45.7 %collective-permute-start.2 = (bf16[16,8,8192]{2,1,0:T(8,128)(2,1)}, bf16[16,8,8192]{2,1,0:T(8,128)(2,1)}, u32[]{:S(2)}, u32[]{:S(2)}) collective-permute-start(bf16[16,8,8192]{2,1,0:T(8,128)(2,1)} %broadcast_select_fusion), channel_id=1, source_target_pairs={{16,0},{32,16},{48,32},{64,48},{80,64},{96,80},{112,96},{128,112},... | collective-permute-start | bytes 6291464 | tf_op jit(solution)/shard_map/ppermute | solution.py:17
  15.6 620.6 %reduce-scatter.2.cloned.1.call-start = ((), (), s32[]{:S(2)}) async-start(), calls=%async_computation.1 | async-start | bytes 2228224 | tf_op jit(solution)/shard_map/reduce_scatter | solution.py:162
  166.4 17.9 %collective-permute-start.1 = (bf16[8,8192]{1,0:T(8,128)(2,1)}, bf16[8,8192]{1,0:T(8,128)(2,1)S(1)}, u32[]{:S(2)}, u32[]{:S(2)}) collective-permute-start(bf16[8,8192]{1,0:T(8,128)(2,1)} %get-tuple-element.486), channel_id=1, source_target_pairs={{16,0},{32,16},{48,32},{64,48},{80,64},{96,80},{112,96},{128,112},... | collective-permute-start | bytes 393224 | tf_op jit(solution)/shard_map/while/body/eval_jaxpr/ppermute | solution.py:17
  192.0 17.9 %collective-permute-start.1 = (bf16[8,8192]{1,0:T(8,128)(2,1)}, bf16[8,8192]{1,0:T(8,128)(2,1)S(1)}, u32[]{:S(2)}, u32[]{:S(2)}) collective-permute-start(bf16[8,8192]{1,0:T(8,128)(2,1)} %get-tuple-element.486), channel_id=1, source_target_pairs={{16,0},{32,16},{48,32},{64,48},{80,64},{96,80},{112,96},{128,112},... | collective-permute-start | bytes 393224 | tf_op jit(solution)/shard_map/while/body/eval_jaxpr/ppermute | solution.py:17
  213.6 18.0 %collective-permute-start = (bf16[8,8192]{1,0:T(8,128)(2,1)}, bf16[8,8192]{1,0:T(8,128)(2,1)S(1)}, u32[]{:S(2)}, u32[]{:S(2)}) collective-permute-start(bf16[8,8192]{1,0:T(8,128)(2,1)} %get-tuple-element.485), channel_id=1, source_target_pairs={{0,16},{16,32},{32,48},{48,64},{64,80},{80,96},{96,112},{112,128},... | collective-permute-start | bytes 393224 | tf_op jit(solution)/shard_map/while/body/eval_jaxpr/ppermute | solution.py:17
  239.8 18.5 %collective-permute-start = (bf16[8,8192]{1,0:T(8,128)(2,1)}, bf16[8,8192]{1,0:T(8,128)(2,1)S(1)}, u32[]{:S(2)}, u32[]{:S(2)}) collective-permute-start(bf16[8,8192]{1,0:T(8,128)(2,1)} %get-tuple-element.485), channel_id=1, source_target_pairs={{0,16},{16,32},{32,48},{48,64},{64,80},{80,96},{96,112},{112,128},... | collective-permute-start | bytes 393224 | tf_op jit(solution)/shard_map/while/body/eval_jaxpr/ppermute | solution.py:17
  245.0 17.9 %collective-permute-start.1 = (bf16[8,8192]{1,0:T(8,128)(2,1)}, bf16[8,8192]{1,0:T(8,128)(2,1)S(1)}, u32[]{:S(2)}, u32[]{:S(2)}) collective-permute-start(bf16[8,8192]{1,0:T(8,128)(2,1)} %get-tuple-element.486), channel_id=1, source_target_pairs={{16,0},{32,16},{48,32},{64,48},{80,64},{96,80},{112,96},{128,112},... | collective-permute-start | bytes 393224 | tf_op jit(solution)/shard_map/while/body/eval_jaxpr/ppermute | solution.py:17
  266.5 18.5 %collective-permute-start = (bf16[8,8192]{1,0:T(8,128)(2,1)}, bf16[8,8192]{1,0:T(8,128)(2,1)S(1)}, u32[]{:S(2)}, u32[]{:S(2)}) collective-permute-start(bf16[8,8192]{1,0:T(8,128)(2,1)} %get-tuple-element.485), channel_id=1, source_target_pairs={{0,16},{16,32},{32,48},{48,64},{64,80},{80,96},{96,112},{112,128},... | collective-permute-start | bytes 393224 | tf_op jit(solution)/shard_map/while/body/eval_jaxpr/ppermute | solution.py:17
  271.7 17.9 %collective-permute-start.1 = (bf16[8,8192]{1,0:T(8,128)(2,1)}, bf16[8,8192]{1,0:T(8,128)(2,1)S(1)}, u32[]{:S(2)}, u32[]{:S(2)}) collective-permute-start(bf16[8,8192]{1,0:T(8,128)(2,1)} %get-tuple-element.486), channel_id=1, source_target_pairs={{16,0},{32,16},{48,32},{64,48},{80,64},{96,80},{112,96},{128,112},... | collective-permute-start | bytes 393224 | tf_op jit(solution)/shard_map/while/body/eval_jaxpr/ppermute | solution.py:17
  293.3 18.5 %collective-permute-start = (bf16[8,8192]{1,0:T(8,128)(2,1)}, bf16[8,8192]{1,0:T(8,128)(2,1)S(1)}, u32[]{:S(2)}, u32[]{:S(2)}) collective-permute-start(bf16[8,8192]{1,0:T(8,128)(2,1)} %get-tuple-element.485), channel_id=1, source_target_pairs={{0,16},{16,32},{32,48},{48,64},{64,80},{80,96},{96,112},{112,128},... | collective-permute-start | bytes 393224 | tf_op jit(solution)/shard_map/while/body/eval_jaxpr/ppermute | solution.py:17
  320.1 18.5 %collective-permute-start = (bf16[8,8192]{1,0:T(8,128)(2,1)}, bf16[8,8192]{1,0:T(8,128)(2,1)S(1)}, u32[]{:S(2)}, u32[]{:S(2)}) collective-permute-start(bf16[8,8192]{1,0:T(8,128)(2,1)} %get-tuple-element.485), channel_id=1, source_target_pairs={{0,16},{16,32},{32,48},{48,64},{64,80},{80,96},{96,112},{112,128},... | collective-permute-start | bytes 393224 | tf_op jit(solution)/shard_map/while/body/eval_jaxpr/ppermute | solution.py:17
  325.3 17.9 %collective-permute-start.1 = (bf16[8,8192]{1,0:T(8,128)(2,1)}, bf16[8,8192]{1,0:T(8,128)(2,1)S(1)}, u32[]{:S(2)}, u32[]{:S(2)}) collective-permute-start(bf16[8,8192]{1,0:T(8,128)(2,1)} %get-tuple-element.486), channel_id=1, source_target_pairs={{16,0},{32,16},{48,32},{64,48},{80,64},{96,80},{112,96},{128,112},... | collective-permute-start | bytes 393224 | tf_op jit(solution)/shard_map/while/body/eval_jaxpr/ppermute | solution.py:17
  346.9 18.5 %collective-permute-start = (bf16[8,8192]{1,0:T(8,128)(2,1)}, bf16[8,8192]{1,0:T(8,128)(2,1)S(1)}, u32[]{:S(2)}, u32[]{:S(2)}) collective-permute-start(bf16[8,8192]{1,0:T(8,128)(2,1)} %get-tuple-element.485), channel_id=1, source_target_pairs={{0,16},{16,32},{32,48},{48,64},{64,80},{80,96},{96,112},{112,128},... | collective-permute-start | bytes 393224 | tf_op jit(solution)/shard_map/while/body/eval_jaxpr/ppermute | solution.py:17
  373.6 18.5 %collective-permute-start = (bf16[8,8192]{1,0:T(8,128)(2,1)}, bf16[8,8192]{1,0:T(8,128)(2,1)S(1)}, u32[]{:S(2)}, u32[]{:S(2)}) collective-permute-start(bf16[8,8192]{1,0:T(8,128)(2,1)} %get-tuple-element.485), channel_id=1, source_target_pairs={{0,16},{16,32},{32,48},{48,64},{64,80},{80,96},{96,112},{112,128},... | collective-permute-start | bytes 393224 | tf_op jit(solution)/shard_map/while/body/eval_jaxpr/ppermute | solution.py:17
  400.4 18.5 %collective-permute-start = (bf16[8,8192]{1,0:T(8,128)(2,1)}, bf16[8,8192]{1,0:T(8,128)(2,1)S(1)}, u32[]{:S(2)}, u32[]{:S(2)}) collective-permute-start(bf16[8,8192]{1,0:T(8,128)(2,1)} %get-tuple-element.485), channel_id=1, source_target_pairs={{0,16},{16,32},{32,48},{48,64},{64,80},{80,96},{96,112},{112,128},... | collective-permute-start | bytes 393224 | tf_op jit(solution)/shard_map/while/body/eval_jaxpr/ppermute | solution.py:17
  405.6 17.9 %collective-permute-start.1 = (bf16[8,8192]{1,0:T(8,128)(2,1)}, bf16[8,8192]{1,0:T(8,128)(2,1)S(1)}, u32[]{:S(2)}, u32[]{:S(2)}) collective-permute-start(bf16[8,8192]{1,0:T(8,128)(2,1)} %get-tuple-element.486), channel_id=1, source_target_pairs={{16,0},{32,16},{48,32},{64,48},{80,64},{96,80},{112,96},{128,112},... | collective-permute-start | bytes 393224 | tf_op jit(solution)/shard_map/while/body/eval_jaxpr/ppermute | solution.py:17
  427.2 18.5 %collective-permute-start = (bf16[8,8192]{1,0:T(8,128)(2,1)}, bf16[8,8192]{1,0:T(8,128)(2,1)S(1)}, u32[]{:S(2)}, u32[]{:S(2)}) collective-permute-start(bf16[8,8192]{1,0:T(8,128)(2,1)} %get-tuple-element.485), channel_id=1, source_target_pairs={{0,16},{16,32},{32,48},{48,64},{64,80},{80,96},{96,112},{112,128},... | collective-permute-start | bytes 393224 | tf_op jit(solution)/shard_map/while/body/eval_jaxpr/ppermute | solution.py:17
  432.4 17.9 %collective-permute-start.1 = (bf16[8,8192]{1,0:T(8,128)(2,1)}, bf16[8,8192]{1,0:T(8,128)(2,1)S(1)}, u32[]{:S(2)}, u32[]{:S(2)}) collective-permute-start(bf16[8,8192]{1,0:T(8,128)(2,1)} %get-tuple-element.486), channel_id=1, source_target_pairs={{16,0},{32,16},{48,32},{64,48},{80,64},{96,80},{112,96},{128,112},... | collective-permute-start | bytes 393224 | tf_op jit(solution)/shard_map/while/body/eval_jaxpr/ppermute | solution.py:17
  453.9 18.5 %collective-permute-start = (bf16[8,8192]{1,0:T(8,128)(2,1)}, bf16[8,8192]{1,0:T(8,128)(2,1)S(1)}, u32[]{:S(2)}, u32[]{:S(2)}) collective-permute-start(bf16[8,8192]{1,0:T(8,128)(2,1)} %get-tuple-element.485), channel_id=1, source_target_pairs={{0,16},{16,32},{32,48},{48,64},{64,80},{80,96},{96,112},{112,128},... | collective-permute-start | bytes 393224 | tf_op jit(solution)/shard_map/while/body/eval_jaxpr/ppermute | solution.py:17
  459.1 17.9 %collective-permute-start.1 = (bf16[8,8192]{1,0:T(8,128)(2,1)}, bf16[8,8192]{1,0:T(8,128)(2,1)S(1)}, u32[]{:S(2)}, u32[]{:S(2)}) collective-permute-start(bf16[8,8192]{1,0:T(8,128)(2,1)} %get-tuple-element.486), channel_id=1, source_target_pairs={{16,0},{32,16},{48,32},{64,48},{80,64},{96,80},{112,96},{128,112},... | collective-permute-start | bytes 393224 | tf_op jit(solution)/shard_map/while/body/eval_jaxpr/ppermute | solution.py:17
  480.7 18.5 %collective-permute-start = (bf16[8,8192]{1,0:T(8,128)(2,1)}, bf16[8,8192]{1,0:T(8,128)(2,1)S(1)}, u32[]{:S(2)}, u32[]{:S(2)}) collective-permute-start(bf16[8,8192]{1,0:T(8,128)(2,1)} %get-tuple-element.485), channel_id=1, source_target_pairs={{0,16},{16,32},{32,48},{48,64},{64,80},{80,96},{96,112},{112,128},... | collective-permute-start | bytes 393224 | tf_op jit(solution)/shard_map/while/body/eval_jaxpr/ppermute | solution.py:17
  485.9 17.9 %collective-permute-start.1 = (bf16[8,8192]{1,0:T(8,128)(2,1)}, bf16[8,8192]{1,0:T(8,128)(2,1)S(1)}, u32[]{:S(2)}, u32[]{:S(2)}) collective-permute-start(bf16[8,8192]{1,0:T(8,128)(2,1)} %get-tuple-element.486), channel_id=1, source_target_pairs={{16,0},{32,16},{48,32},{64,48},{80,64},{96,80},{112,96},{128,112},... | collective-permute-start | bytes 393224 | tf_op jit(solution)/shard_map/while/body/eval_jaxpr/ppermute | solution.py:17
  (21 other events, 354.7 us)
Sparse Core Ops, SparseCore 0:
  10.7 47.2 all-gather.4
  60.1 71.4 all-gather.6
  527.6 108.5 reduce-scatter.1
where the time goes:
time: 651 us; the launch traced here: 644 us
  waiting for transfers between devices  202 us (31%)
  loops' own time  132 us (20%)
  other arithmetic  105 us (16%)
  starting transfers between devices  94.1 us (14%)
  matrix products  49.2 us (8%)
  local copies, waits for them, and re-layouts  41.2 us (6%)
  between operations  21.6 us (3%)
    another operation x1, loops' own time, per_device(): lax.scan(middle_tick, (sent_delta, returned), jnp.arange(1, K - 1, dtype=...  132 us
    reduce_scatter x1, waiting for transfers between devices, per_device(): lax.psum_scatter(partial_value.astype(jnp.bfloat16), 'dp', scatter_dimens...  108 us
    ppermute x31, starting transfers between devices, passed_along(): return lax.ppermute(x, axis, pairs)  94 us
    all_gather x1, waiting for transfers between devices, per_device(): lax.all_gather(up_weight[0], 'dp', axis=1, tiled=True)  68.3 us
    reduce_sum x31, other arithmetic, norm_rows(): jnp.mean(widened * widened, axis=-1, keepdims=True) + EPSILON  34.5 us
    all_gather x1, waiting for transfers between devices, per_device(): lax.all_gather(down_weight[0], 'dp', axis=0, tiled=True)  25.2 us
    convert_element_type x30, other arithmetic, quantize(): return restored.reshape(values.shape).astype(jnp.bfloat16)  23.9 us
    dynamic_update_slice x42, other arithmetic, per_device(): lax.scan(middle_tick, (sent_delta, returned), jnp.arange(1, K - 1, dtype=...  20.4 us
  transfers between devices with their start and end apart: 34, of which 3 were waited for; matrix products, arithmetic and copies ran while one was open for 20% of the time, Pallas kernels for 0%

commit v1 on v0

v1 whole, which is shorter than its diff:
```python
import functools

import jax
import jax.numpy as jnp
from jax import lax
from jax.experimental import pallas as pl
from jax.experimental.pallas import tpu as pltpu
from jax.sharding import PartitionSpec as P

EPSILON = 1e-05
PARTS = 16
FOLD = 4
CHUNKS = 4
LANES = 512
ROWS = 8
RANK = 64
SCALE = 1024.0
NT = (((1,), (1,)), ((), ()))
TN = (((0,), (0,)), ((), ()))
NN = (((1,), (0,)), ((), ()))


def dot(a, b, dims):
    return lax.dot_general(a, b, dims, preferred_element_type=jnp.float32)


def bounds(exponent):
    return jnp.where(
        exponent == -7,
        127.0 * 2.0**-7,
        jnp.where(exponent == -6, 127.0 * 2.0**-6, jnp.where(exponent == -5, 127.0 * 2.0**-5, 127.0 * 2.0**-4)),
    ).astype(jnp.float32)


def spread(table, c):
    per = LANES // 128
    groups = []
    for q in range(FOLD):
        first = q * CHUNKS * per + c * per
        groups.append(
            jnp.concatenate(
                [jnp.broadcast_to(table[:, b : b + 1], (ROWS, 128)) for b in range(first, first + per)], axis=1
            )
        )
    return jnp.concatenate(groups, axis=0)


def clip_to(values, bound):
    return jnp.minimum(jnp.maximum(values, -bound), bound)


def fold_rows(ref, index, c):
    width = CHUNKS * LANES
    parts = []
    for q in range(FOLD):
        lanes = pl.ds(q * width + c * LANES, LANES)
        part = ref[:, lanes] if index is None else ref[index, :, lanes]
        parts.append(part.astype(jnp.float32))
    return jnp.concatenate(parts, axis=0)


def low_half():
    return lax.broadcasted_iota(jnp.int32, (ROWS, 128), 1) < RANK


def gather_groups(product):
    low = low_half()
    first = jnp.where(low, product[0:8, 0:128], product[8:16, 0:128])
    second = jnp.where(low, product[16:24, 128:256], product[24:32, 128:256])
    half = first + second
    return half + pltpu.roll(half, RANK, 1)


def scatter_groups(values):
    low = low_half()
    zero = jnp.zeros_like(values)
    left = jnp.where(low, values, zero)
    right = jnp.where(low, zero, values)
    first = jnp.concatenate([left, right, zero, zero], axis=0)
    second = jnp.concatenate([zero, zero, left, right], axis=0)
    return jnp.concatenate([first, second], axis=1).astype(jnp.bfloat16)


def lane_total(values):
    return jnp.broadcast_to(jnp.sum(values, axis=1, keepdims=True), (ROWS, 128))


def squares(x):
    total = jnp.zeros((ROWS, 128), jnp.float32)
    for q in range(FOLD):
        for i in range(LANES // 128):
            piece = x[q * ROWS : (q + 1) * ROWS, i * 128 : (i + 1) * 128]
            total = total + piece * piece
    return total


def kernel(
    ticks,
    sections,
    slots,
    stored_hbm,
    incoming,
    delta_exp,
    grad_exp,
    gain,
    down,
    up,
    down_out,
    up_out,
    delta_out,
    stored,
    weights,
    forward_in,
    forward_out,
    backward_in,
    backward_out,
    shares_out,
    shares_in,
    exps_in,
    copy_out,
    copy_in,
    x_now,
    back_now,
    stats,
    totals,
    stored_sem,
    weight_send,
    weight_recv,
    forward_send,
    forward_recv,
    backward_send,
    backward_recv,
    share_send,
    share_recv,
    side_send,
    side_recv,
):
    section = lax.axis_index("section")
    me = lax.axis_index("dp")
    is_first = section == 0
    is_last = section == sections - 1
    features = gain.shape[1]

    load_stored = pltpu.make_async_copy(stored_hbm, stored, stored_sem)
    load_stored.start()

    barrier = pltpu.get_barrier_semaphore()

    def peer(offset):
        return lax.rem(me + offset, PARTS)

    for offset in range(1, PARTS):
        pl.semaphore_signal(barrier, inc=1, device_id={"dp": peer(offset)})

    @pl.when(jnp.logical_not(is_first))
    def _():
        pl.semaphore_signal(barrier, inc=1, device_id={"section": section - 1})

    @pl.when(jnp.logical_not(is_last))
    def _():
        pl.semaphore_signal(barrier, inc=1, device_id={"section": section + 1})

    group = me // CHUNKS
    chunk = lax.rem(me, CHUNKS)
    group_rows = pl.ds(pl.multiple_of(group * RANK, RANK), RANK)
    own_lanes = pl.ds(pl.multiple_of(me * LANES, LANES), LANES)
    own_gain = gain[:, own_lanes]
    weights[0, chunk, group_rows, :] = (down[...].astype(jnp.float32) * (own_gain * (1.0 / SCALE))).astype(jnp.bfloat16)
    weights[1, chunk, group_rows, :] = up[...]
    totals[...] = jnp.zeros_like(totals)

    ends = jnp.where(is_first, 1, 0) + jnp.where(is_last, 1, 0)
    pl.semaphore_wait(barrier, PARTS + 1 - ends)

    def weight_copy(which, offset):
        block = weights.at[which, chunk, group_rows, :]
        return pltpu.make_async_remote_copy(
            src_ref=block,
            dst_ref=block,
            send_sem=weight_send.at[which, offset],
            recv_sem=weight_recv.at[which, me],
            device_id={"dp": peer(offset)},
        )

    def weight_arrival(which, offset):
        source = peer(offset)
        rows = pl.ds(pl.multiple_of((source // CHUNKS) * RANK, RANK), RANK)
        block = weights.at[which, lax.rem(source, CHUNKS), rows, :]
        return pltpu.make_async_remote_copy(
            src_ref=block,
            dst_ref=block,
            send_sem=weight_send.at[which, offset],
            recv_sem=weight_recv.at[which, source],
            device_id={"dp": source},
        )

    for which in range(2):
        for offset in range(1, PARTS):
            weight_copy(which, offset).start()

    exps_copy = pltpu.make_async_remote_copy(
        src_ref=delta_exp,
        dst_ref=exps_in,
        send_sem=side_send.at[0],
        recv_sem=side_recv.at[0],
        device_id={"section": section + 1},
    )

    @pl.when(jnp.logical_not(is_last))
    def _():
        exps_copy.start()

    load_stored.wait()

    copy_copy = pltpu.make_async_remote_copy(
        src_ref=copy_out,
        dst_ref=copy_in,
        send_sem=side_send.at[1],
        recv_sem=side_recv.at[1],
        device_id={"section": section - 1},
    )

    @pl.when(jnp.logical_not(is_first))
    def _():
        for c in range(CHUNKS):
            copy_out[c] = fold_rows(stored, slots[ticks], c).astype(jnp.bfloat16)
        copy_copy.start()

    @pl.when(jnp.logical_not(is_last))
    def _():
        for c in range(CHUNKS):
            backward_in[0, c] = fold_rows(incoming, None, c).astype(jnp.bfloat16)

    for offset in range(1, PARTS):
        weight_arrival(0, offset).wait_recv()

    def row_stats(product, total):
        inverse = lax.rsqrt(lane_total(total) * (1.0 / features) + EPSILON)
        before = gather_groups(product) * (inverse * SCALE)
        gate = 1.0 / (1.0 + jnp.exp(-before))
        return inverse, before, gate

    def keep_stats(inverse, before, gate):
        stats[0] = inverse
        stats[1] = before
        stats[2] = gate * (1.0 + before * (1.0 - gate))
        stats[3] = before * gate

    def prepare(tick):
        product = jnp.zeros((FOLD * ROWS, FOLD * RANK), jnp.float32)
        total = jnp.zeros((ROWS, 128), jnp.float32)
        for c in range(CHUNKS):
            rows = fold_rows(stored, slots[ticks + 1 + tick], c)
            narrow = rows.astype(jnp.bfloat16)
            back_now[c] = narrow
            product = product + dot(narrow, weights[0, c], NT)
            total = total + squares(rows)
        keep_stats(*row_stats(product, total))

    @pl.when(jnp.logical_not(is_last))
    def _():
        prepare(0)

    def forward_copy(tick, c):
        return pltpu.make_async_remote_copy(
            src_ref=forward_out.at[tick, c],
            dst_ref=forward_in.at[tick, c],
            send_sem=forward_send.at[tick, c],
            recv_sem=forward_recv.at[tick, c],
            device_id={"section": section + 1},
        )

    def backward_copy(tick, c):
        return pltpu.make_async_remote_copy(
            src_ref=backward_out.at[tick, c],
            dst_ref=backward_in.at[tick, c],
            send_sem=backward_send.at[tick, c],
            recv_sem=backward_recv.at[tick, c],
            device_id={"section": section - 1},
        )

    def forward(tick):
        product = jnp.zeros((FOLD * ROWS, FOLD * RANK), jnp.float32)
        total = jnp.zeros((ROWS, 128), jnp.float32)
        arrives = jnp.logical_and(tick > 0, jnp.logical_not(is_first))
        for c in range(CHUNKS):

            @pl.when(arrives)
            def _(c=c):
                forward_copy(tick, c).wait_recv()
                base = fold_rows(stored, slots[tick], c)
                bound = spread(bounds(exps_in[tick - 1]), c)
                step = clip_to(forward_in[tick, c].astype(jnp.float32) - base, bound)
                x_now[c] = (base + step.astype(jnp.bfloat16).astype(jnp.float32)).astype(jnp.bfloat16)

            @pl.when(jnp.logical_not(arrives))
            def _(c=c):
                x_now[c] = fold_rows(stored, slots[tick], c).astype(jnp.bfloat16)

            x = x_now[c]
            product = product + dot(x, weights[0, c], NT)
            total = total + squares(x.astype(jnp.float32))
        inverse, before, gate = row_stats(product, total)
        hidden = scatter_groups(before * gate)

        @pl.when(is_last)
        def _():
            keep_stats(inverse, before, gate)
            back_now[...] = x_now[...]

        @pl.when(tick == 0)
        def _():
            for offset in range(1, PARTS):
                weight_arrival(1, offset).wait_recv()

        for c in range(CHUNKS):
            output = x_now[c].astype(jnp.float32) + dot(hidden, weights[1, c], NN)

            @pl.when(jnp.logical_and(tick < ticks - 1, jnp.logical_not(is_last)))
            def _(c=c, output=output):
                forward_out[tick + 1, c] = output.astype(jnp.bfloat16)
                forward_copy(tick + 1, c).start()

            @pl.when(is_last)
            def _(c=c, output=output):
                distance = output - fold_rows(stored, slots[tick], c)
                backward_in[tick, c] = distance.astype(jnp.bfloat16)

            @pl.when(tick == ticks - 1)
            def _(c=c, output=output):
                @pl.when(is_last)
                def _():
                    copy_in[c] = fold_rows(stored, slots[tick], c).astype(jnp.bfloat16)

                distance = output - copy_in[c].astype(jnp.float32)
                delta = clip_to(distance, spread(bounds(delta_exp[tick]), c)).astype(jnp.bfloat16)
                for q in range(FOLD):
                    lanes = pl.ds(q * CHUNKS * LANES + c * LANES, LANES)
                    delta_out[:, lanes] = delta[q * ROWS : (q + 1) * ROWS]

    def share_copy(tick, offset):
        return pltpu.make_async_remote_copy(
            src_ref=shares_out.at[tick, peer(offset)],
            dst_ref=shares_in.at[tick, me],
            send_sem=share_send.at[tick],
            recv_sem=share_recv.at[tick],
            device_id={"dp": peer(offset)},
        )

    def all_shares(tick):
        return pltpu.make_async_remote_copy(
            src_ref=shares_out.at[tick, pl.ds(0, PARTS - 1)],
            dst_ref=shares_in.at[tick, pl.ds(0, PARTS - 1)],
            send_sem=share_send.at[tick],
            recv_sem=share_recv.at[tick],
            device_id={"dp": peer(1)},
        )

    def backward(tick):
        product = jnp.zeros((FOLD * ROWS, FOLD * RANK), jnp.float32)
        arrives = jnp.logical_and(tick > 0, jnp.logical_not(is_last))
        for c in range(CHUNKS):

            @pl.when(arrives)
            def _(c=c):
                backward_copy(tick, c).wait_recv()

            product = product + dot(backward_in[tick, c], weights[1, c], NT)
        inverse = stats[0]
        slope = gather_groups(product) * stats[2] * inverse
        pull = lane_total(slope * stats[1]) * (0.5 / features) * inverse
        pull = jnp.concatenate([jnp.concatenate([pull] * (LANES // 128), axis=1)] * FOLD, axis=0)
        spread_slope = scatter_groups(slope * SCALE)

        @pl.when(jnp.logical_and(tick < ticks - 1, jnp.logical_not(is_first)))
        def _():
            for c in range(CHUNKS):
                through = dot(spread_slope, weights[0, c], NN)
                result = backward_in[tick, c].astype(jnp.float32) + through - back_now[c].astype(jnp.float32) * pull
                bound = spread(bounds(grad_exp[tick]), c)
                backward_out[tick + 1, c] = clip_to(result, bound).astype(jnp.bfloat16)
                backward_copy(tick + 1, c).start()

        low = low_half()
        zero = jnp.zeros((ROWS, 128), jnp.float32)
        tail = jnp.concatenate([jnp.where(low, slope, zero), jnp.where(low, zero, stats[3])], axis=0).astype(jnp.bfloat16)
        for c in range(CHUNKS):
            back = back_now[c].astype(jnp.float32)
            cotangent = backward_in[tick, c].astype(jnp.float32)
            for q in range(FOLD):
                rows = slice(q * ROWS, (q + 1) * ROWS)
                pair = jnp.concatenate([back[rows], cotangent[rows]], axis=0)
                shares_out[tick, q * CHUNKS + c, :, 0:LANES] = pair.astype(jnp.bfloat16)
                shares_out[tick, q * CHUNKS + c, :, LANES : LANES + 128] = tail
        for offset in range(1, PARTS):
            share_copy(tick, offset).start()
        shares_in[tick, me] = shares_out[tick, me]

    def add_shares(tick):
        all_shares(tick).wait_recv()
        both = shares_in[tick].reshape(PARTS * 2 * ROWS, LANES + 128)
        totals[...] += dot(both[:, LANES:], both[:, :LANES], TN)

    def one_tick(tick, carry):
        forward(tick)
        backward(tick)

        @pl.when(jnp.logical_and(tick < ticks - 1, jnp.logical_not(is_last)))
        def _():
            prepare(tick + 1)

        @pl.when(tick == 0)
        def _():
            @pl.when(jnp.logical_not(is_first))
            def _():
                exps_copy.wait_recv()

            @pl.when(jnp.logical_not(is_last))
            def _():
                copy_copy.wait_recv()

        @pl.when(tick >= 2)
        def _():
            add_shares(tick - 2)

        return carry

    lax.fori_loop(0, ticks, one_tick, 0)
    add_shares(ticks - 2)
    add_shares(ticks - 1)

    factor = 1.0 / (ticks * ROWS)
    down_out[...] = (totals[0:RANK] * (own_gain * factor)).astype(jnp.bfloat16)
    up_out[...] = (totals[RANK : 2 * RANK] * factor).astype(jnp.bfloat16)

    for which in range(2):
        for offset in range(1, PARTS):
            weight_copy(which, offset).wait_send()

    @pl.when(jnp.logical_not(is_last))
    def _():
        exps_copy.wait_send()

        def drain(tick, carry):
            for c in range(CHUNKS):
                forward_copy(tick, c).wait_send()
            return carry

        lax.fori_loop(1, ticks, drain, 0)

    @pl.when(jnp.logical_not(is_first))
    def _():
        copy_copy.wait_send()

        def drain(tick, carry):
            for c in range(CHUNKS):
                backward_copy(tick, c).wait_send()
            return carry

        lax.fori_loop(1, ticks, drain, 0)

    def drain_shares(tick, carry):
        all_shares(tick).wait_send()
        return carry

    lax.fori_loop(0, ticks, drain_shares, 0)


def per_device(stored_inputs, slot_ids, incoming, delta_exp, grad_exp, norm_gain, down_weight, up_weight):
    stored = stored_inputs[0, 0]
    ticks = delta_exp.shape[2]
    sections = lax.axis_size("section")
    slot_count, rows, features = stored.shape
    message = (CHUNKS, FOLD * ROWS, LANES)
    bf16, f32 = jnp.bfloat16, jnp.float32
    vmem = pl.BlockSpec(memory_space=pltpu.VMEM)
    down_grad, up_grad, delta = pl.pallas_call(
        functools.partial(kernel, ticks, sections),
        out_shape=(
            jax.ShapeDtypeStruct((RANK, LANES), bf16),
            jax.ShapeDtypeStruct((RANK, LANES), bf16),
            jax.ShapeDtypeStruct((rows, features), bf16),
        ),
        in_specs=[pl.BlockSpec(memory_space=pltpu.SMEM), pl.BlockSpec(memory_space=pl.ANY)] + [vmem] * 6,
        out_specs=(vmem, vmem, vmem),
        scratch_shapes=[
            pltpu.VMEM((slot_count, rows, features), bf16),
            pltpu.VMEM((2, CHUNKS, FOLD * RANK, LANES), bf16),
            pltpu.VMEM((ticks,) + message, bf16),
            pltpu.VMEM((ticks,) + message, bf16),
            pltpu.VMEM((ticks,) + message, bf16),
            pltpu.VMEM((ticks,) + message, bf16),
            pltpu.VMEM((ticks, PARTS, 2 * ROWS, LANES + 128), bf16),
            pltpu.VMEM((ticks, PARTS, 2 * ROWS, LANES + 128), bf16),
            pltpu.VMEM(delta_exp.shape[2:], jnp.int32),
            pltpu.VMEM(message, bf16),
            pltpu.VMEM(message, bf16),
            pltpu.VMEM(message, bf16),
            pltpu.VMEM(message, bf16),
            pltpu.VMEM((4, ROWS, 128), f32),
            pltpu.VMEM((2 * RANK, LANES), f32),
            pltpu.SemaphoreType.DMA,
            pltpu.SemaphoreType.DMA((2, PARTS)),
            pltpu.SemaphoreType.DMA((2, PARTS)),
            pltpu.SemaphoreType.DMA((ticks, CHUNKS)),
            pltpu.SemaphoreType.DMA((ticks, CHUNKS)),
            pltpu.SemaphoreType.DMA((ticks, CHUNKS)),
            pltpu.SemaphoreType.DMA((ticks, CHUNKS)),
            pltpu.SemaphoreType.DMA((ticks,)),
            pltpu.SemaphoreType.DMA((ticks,)),
            pltpu.SemaphoreType.DMA((2,)),
            pltpu.SemaphoreType.DMA((2,)),
        ],
        compiler_params=pltpu.CompilerParams(
            collective_id=0, has_side_effects=True, vmem_limit_bytes=52 * 1024 * 1024
        ),
        name="relay",
    )(
        slot_ids[0, 0],
        stored,
        incoming[0, 0],
        delta_exp[0, 0],
        grad_exp[0, 0],
        norm_gain,
        down_weight[0].T,
        up_weight[0],
    )
    return down_grad.T[None], up_grad[None], delta[None, None]


def solution(mesh):
    return jax.shard_map(
        per_device,
        mesh=mesh,
        in_specs=(
            P("section", "dp", None, None, None),
            P("section", "dp", None),
            P("section", "dp", None, None),
            P("section", "dp", None, None, None),
            P("section", "dp", None, None, None),
            P("section", None),
            P("section", "dp", None),
            P("section", None, "dp"),
        ),
        out_specs=(
            P("section", "dp", None),
            P("section", None, "dp"),
            P("section", "dp", None, None),
        ),
        check_vma=False,
    )
```

time: 651 us -> 151 us (0.23)
  waiting for transfers between devices: 202 us -> 0 us
  Pallas kernels: 0 us -> 142 us
  loops' own time: 132 us -> 0 us
  other arithmetic: 105 us -> 0 us
  starting transfers between devices: 94.1 us -> 0 us
  matrix products: 49.2 us -> 0 us
  local copies, waits for them, and re-layouts: 41.2 us -> 7.57 us
  between operations: 21.6 us -> 0.66 us
    pallas_call x0 -> x1, Pallas kernels: none -> 142 us  [per_device(): pl.pallas_call(functools.partial(kernel, ticks, sections), out_shape=(jax...]
    another operation x1 -> x0, loops' own time: 132 us -> none  [per_device(): lax.scan(middle_tick, (sent_delta, returned), jnp.arange(1, K - 1, dtype=...]
    reduce_scatter x1 -> x0, waiting for transfers between devices: 108 us -> none  [per_device(): lax.psum_scatter(partial_value.astype(jnp.bfloat16), 'dp', scatter_dimens...]
    ppermute x31 -> x0, starting transfers between devices: 94 us -> none  [passed_along(): return lax.ppermute(x, axis, pairs)]
    all_gather x2 -> x0, waiting for transfers between devices: 93.5 us -> none  [the longest x1 68.3 us: per_device(): lax.all_gather(up_weight[0], 'dp', axis=1, tiled=True)]
    dot_general x65 -> x0, matrix products: 49.2 us -> none  [the longest x16 19.4 us: process(): jnp.dot(hidden, up_full, preferred_element_type=jnp.float32)]
    reduce_sum x31 -> x0, other arithmetic: 34.5 us -> none  [norm_rows(): jnp.mean(widened * widened, axis=-1, keepdims=True) + EPSILON]
    convert_element_type x49 -> x0, other arithmetic: 28.6 us -> none  [the longest x30 23.9 us: quantize(): return restored.reshape(values.shape).astype(jnp.bfloat16)]
  transfers between devices with their start and end apart: 34 -> 0, of which waited for: 3 -> 0; matrix products, arithmetic and copies ran while one was open for 20% -> 0% of each run, Pallas kernels for 0% -> 0%
where the time goes in v1:
time: 151 us; the launch traced here: 150 us
  Pallas kernels  142 us (94%)
  local copies, waits for them, and re-layouts  7.57 us (5%)
    pallas_call x1, Pallas kernels, per_device(): pl.pallas_call(functools.partial(kernel, ticks, sections), out_shape=(jax...  142 us
    unnamed x17, local copies, waits for them, and re-layouts  7.57 us

profile of v1, /device:TPU:1, one launch (start us, length us, event | category | flops | bytes accessed | tf_op | source)
XLA Modules:
  0.0 150.4 jit_solution(17572038167725525581)
XLA Ops:
  0.6 0.0 copy-start
  0.6 0.9 copy-done
  1.5 0.0 copy-start.1
  1.5 0.8 copy-done.1
  2.4 0.0 copy-start.2
  2.4 0.8 copy-done.2
  3.2 0.0 copy-start.3
  3.2 0.8 copy-done.3
  4.1 0.0 copy-start.4
  4.1 0.8 copy-done.4
  4.9 0.0 copy-start.5
  4.9 0.8 copy-done.5
  5.6 0.0 copy-start.6
  5.6 0.7 copy-done.6
  6.3 142.2 %relay.1 = (bf16[64,512]{1,0:T(8,128)(2,1)S(1)}, bf16[64,512]{1,0:T(8,128)(2,1)S(1)}, bf16[8,8192]{1,0:T(8,128)(2,1)S(1)}) custom-call(s32[33]{0:T(128)S(1)} %bitcast.22, bf16[33,8,8192]{2,1,0:T(8,128)(2,1)} %bitcast.23, bf16[8,8192]{1,0:T(8,128)(2,1)S(1)} %bitcast.14, s32[16,8,64]{2,1,0:T(8,128)S(1)} %bitcast.16, s32[15,8,64]{2,1,0:T(8,128)S(1)} %bitcast.21, ...), custom_call_target="tpu_custom_call" | custom-call | tf_op jit(solution)/shard_map/relay/pallas_call | solution.py:477
  148.5 0.6 copy.14
  149.1 0.6 copy.15
  149.8 0.7 copy.16
Async XLA Ops:
  0.6 0.9 copy-start
  1.5 0.8 copy-start.1
  2.4 0.8 copy-start.2
  3.2 0.8 copy-start.3
  4.1 0.8 copy-start.4
  4.9 0.8 copy-start.5
  5.6 0.7 copy-start.6

commit v2 on v1

v2 whole, which is shorter than its diff:
```python
import functools

import jax
import jax.numpy as jnp
from jax import lax
from jax.experimental import pallas as pl
from jax.experimental.pallas import tpu as pltpu
from jax.sharding import PartitionSpec as P

EPSILON = 1e-05
PARTS = 16
CHIPS = 8
FOLD = 4
CHUNKS = 4
LANES = 512
ROWS = 8
RANK = 64
SCALE = 1024.0
NT = (((1,), (1,)), ((), ()))
TN = (((0,), (0,)), ((), ()))
NN = (((1,), (0,)), ((), ()))


def dot(a, b, dims):
    return lax.dot_general(a, b, dims, preferred_element_type=jnp.float32)


def bounds(exponent):
    return jnp.where(
        exponent == -7,
        127.0 * 2.0**-7,
        jnp.where(exponent == -6, 127.0 * 2.0**-6, jnp.where(exponent == -5, 127.0 * 2.0**-5, 127.0 * 2.0**-4)),
    ).astype(jnp.float32)


def spread(table, c):
    per = LANES // 128
    groups = []
    for q in range(FOLD):
        first = q * CHUNKS * per + c * per
        groups.append(
            jnp.concatenate(
                [jnp.broadcast_to(table[:, b : b + 1], (ROWS, 128)) for b in range(first, first + per)], axis=1
            )
        )
    return jnp.concatenate(groups, axis=0)


def clip_to(values, bound):
    return jnp.minimum(jnp.maximum(values, -bound), bound)


def fold_rows(ref, index, c):
    width = CHUNKS * LANES
    parts = []
    for q in range(FOLD):
        lanes = pl.ds(q * width + c * LANES, LANES)
        part = ref[:, lanes] if index is None else ref[index, :, lanes]
        parts.append(part.astype(jnp.float32))
    return jnp.concatenate(parts, axis=0)


def low_half():
    return lax.broadcasted_iota(jnp.int32, (ROWS, 128), 1) < RANK


def gather_groups(product):
    low = low_half()
    first = jnp.where(low, product[0:8, 0:128], product[8:16, 0:128])
    second = jnp.where(low, product[16:24, 128:256], product[24:32, 128:256])
    half = first + second
    return half + pltpu.roll(half, RANK, 1)


def scatter_groups(values):
    low = low_half()
    zero = jnp.zeros_like(values)
    left = jnp.where(low, values, zero)
    right = jnp.where(low, zero, values)
    first = jnp.concatenate([left, right, zero, zero], axis=0)
    second = jnp.concatenate([zero, zero, left, right], axis=0)
    return jnp.concatenate([first, second], axis=1).astype(jnp.bfloat16)


def lane_total(values):
    return jnp.broadcast_to(jnp.sum(values, axis=1, keepdims=True), (ROWS, 128))


def squares(x):
    total = jnp.zeros((ROWS, 128), jnp.float32)
    for q in range(FOLD):
        for i in range(LANES // 128):
            piece = x[q * ROWS : (q + 1) * ROWS, i * 128 : (i + 1) * 128]
            total = total + piece * piece
    return total


def kernel(
    ticks,
    sections,
    slots_hbm,
    stored_hbm,
    incoming_hbm,
    delta_exp_hbm,
    grad_exp_hbm,
    gain_hbm,
    down_hbm,
    up_hbm,
    down_out,
    up_out,
    delta_out,
    slots,
    stored,
    incoming,
    delta_exp,
    grad_exp,
    gain,
    down,
    up,
    weights,
    turned,
    forward_in,
    forward_out,
    backward_in,
    backward_out,
    shares_out,
    shares_in,
    exps_in,
    copy_out,
    copy_in,
    back_rows,
    back_squares,
    back_products,
    stats,
    forward_bound,
    backward_bound,
    totals,
    operand_sem,
    weight_send,
    weight_recv,
    forward_send,
    forward_recv,
    backward_send,
    backward_recv,
    share_send,
    share_recv,
    side_send,
    side_recv,
):
    section = lax.axis_index("section")
    me = lax.axis_index("dp")
    is_first = section == 0
    is_last = section == sections - 1
    not_first = section > 0
    not_last = section < sections - 1
    features = gain.shape[1]

    pairs = (
        (down_hbm, down),
        (up_hbm, up),
        (gain_hbm, gain),
        (delta_exp_hbm, delta_exp),
        (slots_hbm, slots),
        (stored_hbm, stored),
        (grad_exp_hbm, grad_exp),
        (incoming_hbm, incoming),
    )
    loads = [pltpu.make_async_copy(source, target, operand_sem.at[i]) for i, (source, target) in enumerate(pairs)]
    for load in loads:
        load.start()

    barrier = pltpu.get_barrier_semaphore()

    def peer(offset):
        return lax.rem(me + offset, PARTS)

    for offset in range(1, PARTS):
        pl.semaphore_signal(barrier, inc=1, device_id={"dp": peer(offset)})

    @pl.when(not_first)
    def _():
        pl.semaphore_signal(barrier, inc=1, device_id={"section": section - 1})

    @pl.when(not_last)
    def _():
        pl.semaphore_signal(barrier, inc=1, device_id={"section": section + 1})

    core = lax.rem(me, 2)
    chip = me // 2
    mate = me + 1 - 2 * core

    def block(which, owner):
        rows = pl.ds(pl.multiple_of((owner // CHUNKS) * RANK, RANK), RANK)
        return weights.at[which, lax.rem(owner, CHUNKS), rows, :]

    own_lanes = pl.ds(pl.multiple_of(me * LANES, LANES), LANES)
    for i in range(4):
        loads[i].wait()
    own_gain = gain[:, own_lanes]
    block(0, me)[...] = (down[...].astype(jnp.float32) * (own_gain * (1.0 / SCALE))).astype(jnp.bfloat16)
    block(1, me)[...] = up[...]

    ends = jnp.where(is_first, 1, 0) + jnp.where(is_last, 1, 0)
    pl.semaphore_wait(barrier, PARTS + 1 - ends)

    def block_copy(which, owner, send, to):
        return pltpu.make_async_remote_copy(
            src_ref=block(which, owner),
            dst_ref=block(which, owner),
            send_sem=weight_send.at[which, send],
            recv_sem=weight_recv.at[which, owner],
            device_id={"dp": to},
        )

    def chip_copy(which, offset):
        return block_copy(which, me, offset, lax.rem(chip + offset, CHIPS) * 2 + core)

    def mate_copy(which, offset):
        return block_copy(which, lax.rem(chip + CHIPS - offset, CHIPS) * 2 + core, CHIPS + offset, mate)

    def from_mate(which, offset):
        return block_copy(which, lax.rem(chip + CHIPS - offset, CHIPS) * 2 + 1 - core, CHIPS + offset, mate)

    for which in range(2):
        mate_copy(which, 0).start()
        for offset in range(1, CHIPS):
            chip_copy(which, offset).start()

    exps_copy = pltpu.make_async_remote_copy(
        src_ref=delta_exp,
        dst_ref=exps_in,
        send_sem=side_send.at[0],
        recv_sem=side_recv.at[0],
        device_id={"section": section + 1},
    )
    copy_copy = pltpu.make_async_remote_copy(
        src_ref=copy_out,
        dst_ref=copy_in,
        send_sem=side_send.at[1],
        recv_sem=side_recv.at[1],
        device_id={"section": section - 1},
    )

    @pl.when(not_last)
    def _():
        exps_copy.start()

    for load in loads[4:]:
        load.wait()

    @pl.when(not_first)
    def _():
        for c in range(CHUNKS):
            copy_out[c] = fold_rows(stored, slots[ticks], c).astype(jnp.bfloat16)
        copy_copy.start()

    @pl.when(is_last)
    def _():
        for c in range(CHUNKS):
            copy_in[c] = fold_rows(stored, slots[ticks - 1], c).astype(jnp.bfloat16)

    @pl.when(is_first)
    def _():
        exps_in[...] = delta_exp[...]

        def clear(tick, carry):
            forward_in[tick] = jnp.zeros(forward_in.shape[1:], jnp.bfloat16)
            return carry

        lax.fori_loop(0, ticks, clear, 0)

    totals[...] = jnp.zeros_like(totals)
    for c in range(CHUNKS):
        backward_in[0, c] = fold_rows(incoming, None, c).astype(jnp.bfloat16)

    def take_rows(tick, carry):
        slot = slots[jnp.where(tick == ticks, 0, ticks + 1 + tick)]
        total = jnp.zeros((ROWS, 128), jnp.float32)
        for c in range(CHUNKS):
            rows = fold_rows(stored, slot, c)
            back_rows[tick, c] = rows.astype(jnp.bfloat16)
            total = total + squares(rows)
        back_squares[tick] = total
        return carry

    lax.fori_loop(0, ticks + 1, take_rows, 0)

    def spread_back(tick, carry):
        table = bounds(grad_exp[tick])
        for c in range(CHUNKS):
            backward_bound[tick, c] = spread(table, c)
        return carry

    lax.fori_loop(0, ticks - 1, spread_back, 0)

    for offset in range(1, CHIPS):
        mate_copy(0, offset).wait_recv()
        mate_copy(0, offset).start()

    @pl.when(not_first)
    def _():
        exps_copy.wait_recv()

    own_table = bounds(delta_exp[ticks - 1])
    for c in range(CHUNKS):
        forward_bound[0, c] = spread(own_table, c)

    def spread_forward(tick, carry):
        table = bounds(exps_in[tick - 1]) * jnp.where(is_first, 0.0, 1.0)
        for c in range(CHUNKS):
            forward_bound[tick, c] = spread(table, c)
        return carry

    lax.fori_loop(1, ticks, spread_forward, 0)

    for offset in range(CHIPS):
        from_mate(0, offset).wait_recv()

    back_products[...] = jnp.zeros_like(back_products)

    def multiply(c, carry):
        rows = back_rows[:, c].reshape((ticks + 1) * FOLD * ROWS, LANES)
        back_products[...] += dot(rows, weights[0, c], NT)
        return carry

    lax.fori_loop(0, CHUNKS, multiply, 0)

    for offset in range(1, CHIPS):
        mate_copy(1, offset).wait_recv()
        mate_copy(1, offset).start()

    def row_stats(product, total):
        inverse = lax.rsqrt(lane_total(total) * (1.0 / features) + EPSILON)
        before = gather_groups(product) * (inverse * SCALE)
        gate = 1.0 / (1.0 + jnp.exp(-before))
        return inverse, before, gate

    def keep_stats(tick, inverse, before, gate):
        stats[tick, 0] = inverse
        stats[tick, 1] = before
        stats[tick, 2] = gate * (1.0 + before * (1.0 - gate))
        stats[tick, 3] = before * gate

    def back_stats(tick):
        first = tick * FOLD * ROWS
        if not isinstance(tick, int):
            first = pl.multiple_of(first, FOLD * ROWS)
        keep_stats(tick, *row_stats(back_products[pl.ds(first, FOLD * ROWS)], back_squares[tick]))

    back_stats(ticks)

    def four_stats(group, carry):
        for i in range(4):
            back_stats(group * 4 + i)
        return carry

    lax.fori_loop(0, ticks // 4, four_stats, 0)

    for offset in range(CHIPS):
        from_mate(1, offset).wait_recv()

    def forward_copy(tick, c):
        return pltpu.make_async_remote_copy(
            src_ref=forward_out.at[tick, c],
            dst_ref=forward_in.at[tick, c],
            send_sem=forward_send.at[tick, c],
            recv_sem=forward_recv.at[tick, c],
            device_id={"section": section + 1},
        )

    def backward_copy(tick, c):
        return pltpu.make_async_remote_copy(
            src_ref=backward_out.at[tick, c],
            dst_ref=backward_in.at[tick, c],
            send_sem=backward_send.at[tick, c],
            recv_sem=backward_recv.at[tick, c],
            device_id={"section": section - 1},
        )

    def forward(tick, begin, final):
        if begin:
            hidden = stats[ticks, 3]
        else:
            product = jnp.zeros((FOLD * ROWS, FOLD * RANK), jnp.float32)
            total = jnp.zeros((ROWS, 128), jnp.float32)
            for c in range(CHUNKS):

                @pl.when(not_first)
                def _(c=c):
                    forward_copy(tick, c).wait_recv()

                base = fold_rows(stored, slots[tick], c)
                step = clip_to(forward_in[tick, c].astype(jnp.float32) - base, forward_bound[tick, c])
                x = (base + step.astype(jnp.bfloat16).astype(jnp.float32)).astype(jnp.bfloat16)
                back_rows[ticks, c] = x
                product = product + dot(x, turned[0, c], NN)
                total = total + squares(x.astype(jnp.float32))
            inverse, before, gate = row_stats(product, total)
            keep_stats(ticks, inverse, before, gate)
            hidden = before * gate
        hidden = scatter_groups(hidden)
        for c in range(CHUNKS):
            output = back_rows[ticks, c].astype(jnp.float32) + dot(hidden, weights[1, c], NN)
            if final:
                delta = clip_to(output - copy_in[c].astype(jnp.float32), forward_bound[0, c]).astype(jnp.bfloat16)
                for q in range(FOLD):
                    lanes = pl.ds(q * CHUNKS * LANES + c * LANES, LANES)
                    delta_out[:, lanes] = delta[q * ROWS : (q + 1) * ROWS]
            else:
                forward_out[tick + 1, c] = output.astype(jnp.bfloat16)

                @pl.when(not_last)
                def _(c=c):
                    forward_copy(tick + 1, c).start()

        @pl.when(is_last)
        def _():
            for c in range(CHUNKS):
                output = back_rows[ticks, c].astype(jnp.float32) + dot(hidden, weights[1, c], NN)
                distance = output - fold_rows(stored, slots[tick], c)
                backward_in[ticks, c] = distance.astype(jnp.bfloat16)

    def share_copy(pair, offset):
        return pltpu.make_async_remote_copy(
            src_ref=shares_out.at[pair, peer(offset)],
            dst_ref=shares_in.at[pair, me],
            send_sem=share_send.at[pair],
            recv_sem=share_recv.at[pair],
            device_id={"dp": peer(offset)},
        )

    def all_shares(pair):
        return pltpu.make_async_remote_copy(
            src_ref=shares_out.at[pair, pl.ds(0, PARTS - 1)],
            dst_ref=shares_in.at[pair, pl.ds(0, PARTS - 1)],
            send_sem=share_send.at[pair],
            recv_sem=share_recv.at[pair],
            device_id={"dp": peer(1)},
        )

    def backward(tick, begin, final, pair, half):
        here = jnp.where(is_last, ticks, tick)
        product = jnp.zeros((FOLD * ROWS, FOLD * RANK), jnp.float32)
        for c in range(CHUNKS):
            if not begin:

                @pl.when(not_last)
                def _(c=c):
                    backward_copy(tick, c).wait_recv()

            cotangent = backward_in[here, c]
            if begin:
                product = product + dot(cotangent, weights[1, c], NT)
            else:
                product = product + dot(cotangent, turned[1, c], NN)
        inverse = stats[here, 0]
        slope = gather_groups(product) * stats[here, 2] * inverse
        if not final:
            pull = lane_total(slope * stats[here, 1]) * (0.5 / features) * inverse
            pull = jnp.concatenate([jnp.concatenate([pull] * (LANES // 128), axis=1)] * FOLD, axis=0)
            spread_slope = scatter_groups(slope * SCALE)
            for c in range(CHUNKS):
                through = dot(spread_slope, weights[0, c], NN)
                result = backward_in[here, c].astype(jnp.float32) + through
                result = result - back_rows[here, c].astype(jnp.float32) * pull
                backward_out[tick + 1, c] = clip_to(result, backward_bound[tick, c]).astype(jnp.bfloat16)

                @pl.when(not_first)
                def _(c=c):
                    backward_copy(tick + 1, c).start()

        low = low_half()
        zero = jnp.zeros((ROWS, 128), jnp.float32)
        tail = jnp.concatenate([jnp.where(low, slope, zero), jnp.where(low, zero, stats[here, 3])], axis=0)
        tail = tail.astype(jnp.bfloat16)
        for c in range(CHUNKS):
            back = back_rows[here, c].astype(jnp.float32)
            cotangent = backward_in[here, c].astype(jnp.float32)
            for q in range(FOLD):
                rows = slice(q * ROWS, (q + 1) * ROWS)
                both = jnp.concatenate([back[rows], cotangent[rows]], axis=0)
                shares_out[pair, q * CHUNKS + c, half, :, 0:LANES] = both.astype(jnp.bfloat16)
                shares_out[pair, q * CHUNKS + c, half, :, LANES : LANES + 128] = tail

    def send_shares(pair):
        for offset in range(1, PARTS):
            share_copy(pair, offset).start()
        shares_in[pair, me] = shares_out[pair, me]

    def add_shares(pair):
        all_shares(pair).wait_recv()
        both = shares_in[pair].reshape(PARTS * 4 * ROWS, LANES + 128)
        totals[...] += dot(both[:, LANES:], both[:, :LANES], TN)

    forward(0, True, False)
    backward(0, True, False, 0, 0)
    for which in range(2):
        for c in range(CHUNKS):
            turned[which, c] = weights[which, c].T

    def two_ticks(pair, carry):
        tick = 2 * pair + 1
        forward(tick, False, False)
        backward(tick, False, False, pair, 1)
        send_shares(pair)
        forward(tick + 1, False, False)
        backward(tick + 1, False, False, pair + 1, 0)

        @pl.when(pair >= 1)
        def _():
            add_shares(pair - 1)

        return carry

    lax.fori_loop(0, ticks // 2 - 1, two_ticks, 0)

    @pl.when(not_last)
    def _():
        copy_copy.wait_recv()

    forward(ticks - 1, False, True)
    backward(ticks - 1, False, True, ticks // 2 - 1, 1)
    send_shares(ticks // 2 - 1)
    add_shares(ticks // 2 - 2)

    for which in range(2):
        mate_copy(which, 0).wait_send()
        for offset in range(1, CHIPS):
            chip_copy(which, offset).wait_send()
            mate_copy(which, offset).wait_send()

    @pl.when(not_last)
    def _():
        exps_copy.wait_send()

        def drain(tick, carry):
            for c in range(CHUNKS):
                forward_copy(tick, c).wait_send()
            return carry

        lax.fori_loop(1, ticks, drain, 0)

    @pl.when(not_first)
    def _():
        copy_copy.wait_send()

        def drain(tick, carry):
            for c in range(CHUNKS):
                backward_copy(tick, c).wait_send()
            return carry

        lax.fori_loop(1, ticks, drain, 0)

    add_shares(ticks // 2 - 1)
    factor = 1.0 / (ticks * ROWS)
    down_out[...] = (totals[0:RANK] * (own_gain * factor)).astype(jnp.bfloat16)
    up_out[...] = (totals[RANK : 2 * RANK] * factor).astype(jnp.bfloat16)

    def drain_shares(pair, carry):
        all_shares(pair).wait_send()
        return carry

    lax.fori_loop(0, ticks // 2, drain_shares, 0)


def per_device(stored_inputs, slot_ids, incoming, delta_exp, grad_exp, norm_gain, down_weight, up_weight):
    stored = stored_inputs[0, 0]
    ticks = delta_exp.shape[2]
    sections = lax.axis_size("section")
    message = (CHUNKS, FOLD * ROWS, LANES)
    bf16, f32 = jnp.bfloat16, jnp.float32
    vmem = pl.BlockSpec(memory_space=pltpu.VMEM)
    operands = (
        slot_ids[0, 0],
        stored,
        incoming[0, 0],
        delta_exp[0, 0],
        grad_exp[0, 0],
        norm_gain,
        down_weight[0].T,
        up_weight[0],
    )
    shares = (ticks // 2, PARTS, 2, 2 * ROWS, LANES + 128)
    down_grad, up_grad, delta = pl.pallas_call(
        functools.partial(kernel, ticks, sections),
        out_shape=(
            jax.ShapeDtypeStruct((RANK, LANES), bf16),
            jax.ShapeDtypeStruct((RANK, LANES), bf16),
            jax.ShapeDtypeStruct(stored.shape[1:], bf16),
        ),
        in_specs=[pl.BlockSpec(memory_space=pl.ANY)] * len(operands),
        out_specs=(vmem, vmem, vmem),
        scratch_shapes=[pltpu.SMEM(operands[0].shape, jnp.int32)]
        + [pltpu.VMEM(operand.shape, operand.dtype) for operand in operands[1:]]
        + [
            pltpu.VMEM((2, CHUNKS, FOLD * RANK, LANES), bf16),
            pltpu.VMEM((2, CHUNKS, LANES, FOLD * RANK), bf16),
            pltpu.VMEM((ticks,) + message, bf16),
            pltpu.VMEM((ticks,) + message, bf16),
            pltpu.VMEM((ticks + 1,) + message, bf16),
            pltpu.VMEM((ticks,) + message, bf16),
            pltpu.VMEM(shares, bf16),
            pltpu.VMEM(shares, bf16),
            pltpu.VMEM(delta_exp.shape[2:], jnp.int32),
            pltpu.VMEM(message, bf16),
            pltpu.VMEM(message, bf16),
            pltpu.VMEM((ticks + 1,) + message, bf16),
            pltpu.VMEM((ticks + 1, ROWS, 128), f32),
            pltpu.VMEM(((ticks + 1) * FOLD * ROWS, FOLD * RANK), f32),
            pltpu.VMEM((ticks + 1, 4, ROWS, 128), f32),
            pltpu.VMEM((ticks,) + message, f32),
            pltpu.VMEM((ticks - 1,) + message, f32),
            pltpu.VMEM((2 * RANK, LANES), f32),
            pltpu.SemaphoreType.DMA((len(operands),)),
            pltpu.SemaphoreType.DMA((2, 2 * CHIPS)),
            pltpu.SemaphoreType.DMA((2, PARTS)),
            pltpu.SemaphoreType.DMA((ticks, CHUNKS)),
            pltpu.SemaphoreType.DMA((ticks, CHUNKS)),
            pltpu.SemaphoreType.DMA((ticks, CHUNKS)),
            pltpu.SemaphoreType.DMA((ticks, CHUNKS)),
            pltpu.SemaphoreType.DMA((ticks // 2,)),
            pltpu.SemaphoreType.DMA((ticks // 2,)),
            pltpu.SemaphoreType.DMA((2,)),
            pltpu.SemaphoreType.DMA((2,)),
        ],
        compiler_params=pltpu.CompilerParams(
            collective_id=0, has_side_effects=True, vmem_limit_bytes=56 * 1024 * 1024
        ),
        name="relay",
    )(*operands)
    return down_grad.T[None], up_grad[None], delta[None, None]


def solution(mesh):
    return jax.shard_map(
        per_device,
        mesh=mesh,
        in_specs=(
            P("section", "dp", None, None, None),
            P("section", "dp", None),
            P("section", "dp", None, None),
            P("section", "dp", None, None, None),
            P("section", "dp", None, None, None),
            P("section", None),
            P("section", "dp", None),
            P("section", None, "dp"),
        ),
        out_specs=(
            P("section", "dp", None),
            P("section", None, "dp"),
            P("section", "dp", None, None),
        ),
        check_vma=False,
    )
```

time: 151 us -> 141 us (0.934)
  Pallas kernels: 142 us -> 136 us
  local copies, waits for them, and re-layouts: 7.57 us -> 4.51 us
    pallas_call x1, Pallas kernels: 142 us -> 136 us  [per_device(): pl.pallas_call(functools.partial(kernel, ticks, sections), out_shape=(jax...]
    unnamed x17 -> x3, local copies, waits for them, and re-layouts: 7.57 us -> 4.51 us
where the time goes in v2:
time: 141 us
  Pallas kernels  136 us (96%)
  local copies, waits for them, and re-layouts  4.51 us (3%)
    pallas_call x1, Pallas kernels, per_device(): pl.pallas_call(functools.partial(kernel, ticks, sections), out_shape=(jax...  136 us
    unnamed x3, local copies, waits for them, and re-layouts  4.51 us

profile of v2, /device:TPU:1, one launch (start us, length us, event | category | flops | bytes accessed | tf_op | source)
XLA Modules:
  0.0 141.2 jit_solution(3790442071525258068)
XLA Ops:
  0.6 136.1 %relay.1 = (bf16[64,512]{1,0:T(8,128)(2,1)}, bf16[64,512]{1,0:T(8,128)(2,1)}, bf16[8,8192]{1,0:T(8,128)(2,1)}) custom-call(s32[33]{0:T(128)} %bitcast.23, bf16[33,8,8192]{2,1,0:T(8,128)(2,1)} %bitcast.14, bf16[8,8192]{1,0:T(8,128)(2,1)} %bitcast.15, s32[16,8,64]{2,1,0:T(8,128)} %bitcast.17, s32[15,8,64]{2,1,0:T(8,128)} %bitcast.22, f32[1,8192]{1,0:T(1,128)} %gain_hbm.1, ...), custom_call_target="tpu_custom_call" | custom-call | tf_op jit(solution)/shard_map/relay/pallas_call | solution.py:584
  136.7 1.5 %copy.14 = bf16[1,512,64]{1,2,0:T(8,128)(2,1)} copy(bf16[1,512,64]{1,2,0:T(8,128)(2,1)} %bitcast.21) | data formatting | bytes 131072
  138.2 1.5 %copy.15 = bf16[1,64,512]{2,1,0:T(8,128)(2,1)} copy(bf16[1,64,512]{2,1,0:T(8,128)(2,1)} %bitcast.20) | data formatting | bytes 131072
  139.6 1.6 %copy.16 = bf16[1,1,8,8192]{3,2,1,0:T(8,128)(2,1)} copy(bf16[1,1,8,8192]{3,2,1,0:T(8,128)(2,1)} %bitcast.16) | data formatting | bytes 262144

commit v3 on v2

--- a/solution.py
+++ b/solution.py
@@ -23,6 +23,16 @@
 
 def dot(a, b, dims):
     return lax.dot_general(a, b, dims, preferred_element_type=jnp.float32)
+
+
+def dot_in(a, b):
+    half = a.shape[1] // 2
+    return dot(a[:, :half], b[:half], NN), dot(a[:, half:], b[half:], NN)
+
+
+def dot_out(a, b):
+    half = b.shape[1] // 2
+    return jnp.concatenate([dot(a, b[:, :half], NN), dot(a, b[:, half:], NN)], axis=1)
 
 
 def bounds(exponent):
@@ -154,6 +164,9 @@
     not_first = section > 0
     not_last = section < sections - 1
     features = gain.shape[1]
+    is_lower = section < sections // 2
+    is_upper = section >= sections // 2
+    lag = jnp.where(is_lower, 1, 0)
 
     pairs = (
         (down_hbm, down),
@@ -285,13 +298,12 @@
 
     lax.fori_loop(0, ticks + 1, take_rows, 0)
 
-    def spread_back(tick, carry):
+    def spread_back(tick):
         table = bounds(grad_exp[tick])
         for c in range(CHUNKS):
-            backward_bound[tick, c] = spread(table, c)
-        return carry
-
-    lax.fori_loop(0, ticks - 1, spread_back, 0)
+            backward_bound[c] = spread(table, c)
+
+    spread_back(0)
 
     for offset in range(1, CHIPS):
         mate_copy(0, offset).wait_recv()
@@ -301,17 +313,13 @@
     def _():
         exps_copy.wait_recv()
 
-    own_table = bounds(delta_exp[ticks - 1])
-    for c in range(CHUNKS):
-        forward_bound[0, c] = spread(own_table, c)
-
-    def spread_forward(tick, carry):
-        table = bounds(exps_in[tick - 1]) * jnp.where(is_first, 0.0, 1.0)
-        for c in range(CHUNKS):
-            forward_bound[tick, c] = spread(table, c)
-        return carry
-
-    lax.fori_loop(1, ticks, spread_forward, 0)
+    def spread_forward(tick, final):
+        if final:
+            table = bounds(delta_exp[tick])
+        else:
+            table = bounds(exps_in[tick]) * jnp.where(is_first, 0.0, 1.0)
+        for c in range(CHUNKS):
+            forward_bound[1 if final else 0, c] = spread(table, c)
 
     for offset in range(CHIPS):
         from_mate(0, offset).wait_recv()
@@ -381,7 +389,7 @@
         if begin:
             hidden = stats[ticks, 3]
         else:
-            product = jnp.zeros((FOLD * ROWS, FOLD * RANK), jnp.float32)
+            sums = [jnp.zeros((FOLD * ROWS, FOLD * RANK), jnp.float32)] * 2
             total = jnp.zeros((ROWS, 128), jnp.float32)
             for c in range(CHUNKS):
 
@@ -390,23 +398,18 @@
                     forward_copy(tick, c).wait_recv()
 
                 base = fold_rows(stored, slots[tick], c)
-                step = clip_to(forward_in[tick, c].astype(jnp.float32) - base, forward_bound[tick, c])
+                step = clip_to(forward_in[tick, c].astype(jnp.float32) - base, forward_bound[0, c])
                 x = (base + step.astype(jnp.bfloat16).astype(jnp.float32)).astype(jnp.bfloat16)
                 back_rows[ticks, c] = x
-                product = product + dot(x, turned[0, c], NN)
+                sums = [a + b for a, b in zip(sums, dot_in(x, turned[0, c]))]
                 total = total + squares(x.astype(jnp.float32))
-            inverse, before, gate = row_stats(product, total)
+            inverse, before, gate = row_stats(sums[0] + sums[1], total)
             keep_stats(ticks, inverse, before, gate)
             hidden = before * gate
         hidden = scatter_groups(hidden)
-        for c in range(CHUNKS):
-            output = back_rows[ticks, c].astype(jnp.float32) + dot(hidden, weights[1, c], NN)
-            if final:
-                delta = clip_to(output - copy_in[c].astype(jnp.float32), forward_bound[0, c]).astype(jnp.bfloat16)
-                for q in range(FOLD):
-                    lanes = pl.ds(q * CHUNKS * LANES + c * LANES, LANES)
-                    delta_out[:, lanes] = delta[q * ROWS : (q + 1) * ROWS]
-            else:
+        if not final:
+            for c in range(CHUNKS):
+                output = back_rows[ticks, c].astype(jnp.float32) + dot_out(hidden, weights[1, c])
                 forward_out[tick + 1, c] = output.astype(jnp.bfloat16)
 
                 @pl.when(not_last)
@@ -416,9 +419,19 @@
         @pl.when(is_last)
         def _():
             for c in range(CHUNKS):
-                output = back_rows[ticks, c].astype(jnp.float32) + dot(hidden, weights[1, c], NN)
+                output = back_rows[ticks, c].astype(jnp.float32) + dot_out(hidden, weights[1, c])
                 distance = output - fold_rows(stored, slots[tick], c)
                 backward_in[ticks, c] = distance.astype(jnp.bfloat16)
+
+        return hidden
+
+    def give_delta(hidden):
+        for c in range(CHUNKS):
+            output = back_rows[ticks, c].astype(jnp.float32) + dot_out(hidden, weights[1, c])
+            delta = clip_to(output - copy_in[c].astype(jnp.float32), forward_bound[1, c]).astype(jnp.bfloat16)
+            for q in range(FOLD):
+                lanes = pl.ds(q * CHUNKS * LANES + c * LANES, LANES)
+                delta_out[:, lanes] = delta[q * ROWS : (q + 1) * ROWS]
 
     def share_copy(pair, offset):
         return pltpu.make_async_remote_copy(
@@ -438,32 +451,33 @@
             device_id={"dp": peer(1)},
         )
 
-    def backward(tick, begin, final, pair, half):
+    def backward(tick, begin, final):
+        pair, half = tick // 2, lax.rem(tick, 2)
         here = jnp.where(is_last, ticks, tick)
-        product = jnp.zeros((FOLD * ROWS, FOLD * RANK), jnp.float32)
+        sums = [jnp.zeros((FOLD * ROWS, FOLD * RANK), jnp.float32)] * 2
         for c in range(CHUNKS):
             if not begin:
 
-                @pl.when(not_last)
+                @pl.when(jnp.logical_and(not_last, tick > 0))
                 def _(c=c):
                     backward_copy(tick, c).wait_recv()
 
             cotangent = backward_in[here, c]
             if begin:
-                product = product + dot(cotangent, weights[1, c], NT)
+                sums[0] = sums[0] + dot(cotangent, weights[1, c], NT)
             else:
-                product = product + dot(cotangent, turned[1, c], NN)
+                sums = [a + b for a, b in zip(sums, dot_in(cotangent, turned[1, c]))]
         inverse = stats[here, 0]
-        slope = gather_groups(product) * stats[here, 2] * inverse
+        slope = gather_groups(sums[0] + sums[1]) * stats[here, 2] * inverse
         if not final:
             pull = lane_total(slope * stats[here, 1]) * (0.5 / features) * inverse
             pull = jnp.concatenate([jnp.concatenate([pull] * (LANES // 128), axis=1)] * FOLD, axis=0)
             spread_slope = scatter_groups(slope * SCALE)
             for c in range(CHUNKS):
-                through = dot(spread_slope, weights[0, c], NN)
+                through = dot_out(spread_slope, weights[0, c])
                 result = backward_in[here, c].astype(jnp.float32) + through
                 result = result - back_rows[here, c].astype(jnp.float32) * pull
-                backward_out[tick + 1, c] = clip_to(result, backward_bound[tick, c]).astype(jnp.bfloat16)
+                backward_out[tick + 1, c] = clip_to(result, backward_bound[c]).astype(jnp.bfloat16)
 
                 @pl.when(not_first)
                 def _(c=c):
@@ -493,7 +507,13 @@
         totals[...] += dot(both[:, LANES:], both[:, :LANES], TN)
 
     forward(0, True, False)
-    backward(0, True, False, 0, 0)
+
+    @pl.when(is_upper)
+    def _():
+        backward(0, True, False)
+        spread_back(1)
+
+    spread_forward(0, False)
     for which in range(2):
         for c in range(CHUNKS):
             turned[which, c] = weights[which, c].T
@@ -501,10 +521,22 @@
     def two_ticks(pair, carry):
         tick = 2 * pair + 1
         forward(tick, False, False)
-        backward(tick, False, False, pair, 1)
-        send_shares(pair)
+        backward(tick - lag, False, False)
+        spread_forward(tick, False)
+        spread_back(tick + 1 - lag)
+
+        @pl.when(is_upper)
+        def _():
+            send_shares(pair)
+
         forward(tick + 1, False, False)
-        backward(tick + 1, False, False, pair + 1, 0)
+        backward(tick + 1 - lag, False, False)
+        spread_forward(tick + 1, False)
+        spread_back(jnp.minimum(tick + 2 - lag, ticks - 2))
+
+        @pl.when(is_lower)
+        def _():
+            send_shares(pair)
 
         @pl.when(pair >= 1)
         def _():
@@ -518,9 +550,16 @@
     def _():
         copy_copy.wait_recv()
 
-    forward(ticks - 1, False, True)
-    backward(ticks - 1, False, True, ticks // 2 - 1, 1)
+    spread_forward(ticks - 1, True)
+    last_hidden = forward(ticks - 1, False, True)
+
+    @pl.when(is_lower)
+    def _():
+        backward(ticks - 2, False, False)
+
+    backward(ticks - 1, False, True)
     send_shares(ticks // 2 - 1)
+    give_delta(last_hidden)
     add_shares(ticks // 2 - 2)
 
     for which in range(2):
@@ -608,8 +647,8 @@
             pltpu.VMEM((ticks + 1, ROWS, 128), f32),
             pltpu.VMEM(((ticks + 1) * FOLD * ROWS, FOLD * RANK), f32),
             pltpu.VMEM((ticks + 1, 4, ROWS, 128), f32),
-            pltpu.VMEM((ticks,) + message, f32),
-            pltpu.VMEM((ticks - 1,) + message, f32),
+            pltpu.VMEM((2,) + message, f32),
+            pltpu.VMEM(message, f32),
             pltpu.VMEM((2 * RANK, LANES), f32),
             pltpu.SemaphoreType.DMA((len(operands),)),
             pltpu.SemaphoreType.DMA((2, 2 * CHIPS)),

time: 141 us -> 149 us (1.057)
  Pallas kernels: 136 us -> 143 us
    pallas_call x1, Pallas kernels: 136 us -> 143 us  [per_device(): pl.pallas_call(functools.partial(kernel, ticks, sections), out_shape=(jax...]
where the time goes in v3:
time: 149 us
  Pallas kernels  143 us (96%)
  local copies, waits for them, and re-layouts  4.51 us (3%)
    pallas_call x1, Pallas kernels, per_device(): pl.pallas_call(functools.partial(kernel, ticks, sections), out_shape=(jax...  143 us
    unnamed x3, local copies, waits for them, and re-layouts  4.51 us

profile of v3, /device:TPU:1, one launch (start us, length us, event | category | flops | bytes accessed | tf_op | source)
XLA Modules:
  0.0 148.6 jit_solution(4274306418145914973)
XLA Ops:
  0.6 143.4 %relay.1 = (bf16[64,512]{1,0:T(8,128)(2,1)}, bf16[64,512]{1,0:T(8,128)(2,1)}, bf16[8,8192]{1,0:T(8,128)(2,1)}) custom-call(s32[33]{0:T(128)} %bitcast.23, bf16[33,8,8192]{2,1,0:T(8,128)(2,1)} %bitcast.14, bf16[8,8192]{1,0:T(8,128)(2,1)} %bitcast.15, s32[16,8,64]{2,1,0:T(8,128)} %bitcast.17, s32[15,8,64]{2,1,0:T(8,128)} %bitcast.22, f32[1,8192]{1,0:T(1,128)} %gain_hbm.1, ...), custom_call_target="tpu_custom_call" | custom-call | tf_op jit(solution)/shard_map/relay/pallas_call | solution.py:623
  144.1 1.5 copy.14
  145.5 1.5 copy.15
  147.0 1.6 %copy.16 = bf16[1,1,8,8192]{3,2,1,0:T(8,128)(2,1)} copy(bf16[1,1,8,8192]{3,2,1,0:T(8,128)(2,1)} %bitcast.16) | data formatting | bytes 262144

commit v4 on v3

--- a/solution.py
+++ b/solution.py
@@ -145,6 +145,8 @@
     forward_bound,
     backward_bound,
     totals,
+    sums_out,
+    sums_in,
     operand_sem,
     weight_send,
     weight_recv,
@@ -184,11 +186,8 @@
 
     barrier = pltpu.get_barrier_semaphore()
 
-    def peer(offset):
-        return lax.rem(me + offset, PARTS)
-
     for offset in range(1, PARTS):
-        pl.semaphore_signal(barrier, inc=1, device_id={"dp": peer(offset)})
+        pl.semaphore_signal(barrier, inc=1, device_id={"dp": lax.rem(me + offset, PARTS)})
 
     @pl.when(not_first)
     def _():
@@ -433,23 +432,39 @@
                 lanes = pl.ds(q * CHUNKS * LANES + c * LANES, LANES)
                 delta_out[:, lanes] = delta[q * ROWS : (q + 1) * ROWS]
 
-    def share_copy(pair, offset):
+    side = lax.rem(me // 2, 2)
+    number = (me // 4) * 2 + core
+
+    def member(index, on_side):
+        return (index // 2) * 4 + on_side * 2 + lax.rem(index, 2)
+
+    def share_copy(pair, offset, other):
+        to = lax.rem(number + offset, CHIPS)
         return pltpu.make_async_remote_copy(
-            src_ref=shares_out.at[pair, peer(offset)],
-            dst_ref=shares_in.at[pair, me],
+            src_ref=shares_out.at[pair, member(to, 1 - side if other else side)],
+            dst_ref=shares_in.at[pair, other, number],
             send_sem=share_send.at[pair],
             recv_sem=share_recv.at[pair],
-            device_id={"dp": peer(offset)},
+            device_id={"dp": member(to, side)},
         )
 
     def all_shares(pair):
+        seven = shares_in.at[pair, :, pl.ds(0, CHIPS - 1)]
         return pltpu.make_async_remote_copy(
-            src_ref=shares_out.at[pair, pl.ds(0, PARTS - 1)],
-            dst_ref=shares_in.at[pair, pl.ds(0, PARTS - 1)],
+            src_ref=seven,
+            dst_ref=seven,
             send_sem=share_send.at[pair],
             recv_sem=share_recv.at[pair],
-            device_id={"dp": peer(1)},
+            device_id={"dp": member(lax.rem(number + 1, CHIPS), side)},
         )
+
+    sums_copy = pltpu.make_async_remote_copy(
+        src_ref=sums_out,
+        dst_ref=sums_in,
+        send_sem=side_send.at[2],
+        recv_sem=side_recv.at[2],
+        device_id={"dp": member(number, 1 - side)},
+    )
 
     def backward(tick, begin, final):
         pair, half = tick // 2, lax.rem(tick, 2)
@@ -497,14 +512,17 @@
                 shares_out[pair, q * CHUNKS + c, half, :, LANES : LANES + 128] = tail
 
     def send_shares(pair):
-        for offset in range(1, PARTS):
-            share_copy(pair, offset).start()
-        shares_in[pair, me] = shares_out[pair, me]
+        for offset in range(1, CHIPS):
+            for other in range(2):
+                share_copy(pair, offset, other).start()
+        for other in range(2):
+            shares_in[pair, other, number] = shares_out[pair, member(number, 1 - side if other else side)]
 
     def add_shares(pair):
         all_shares(pair).wait_recv()
-        both = shares_in[pair].reshape(PARTS * 4 * ROWS, LANES + 128)
-        totals[...] += dot(both[:, LANES:], both[:, :LANES], TN)
+        for other in range(2):
+            both = shares_in[pair, other].reshape(CHIPS * 4 * ROWS, LANES + 128)
+            totals[other] += dot(both[:, LANES:], both[:, :LANES], TN)
 
     forward(0, True, False)
 
@@ -538,9 +556,9 @@
         def _():
             send_shares(pair)
 
-        @pl.when(pair >= 1)
+        @pl.when(pair >= 2)
         def _():
-            add_shares(pair - 1)
+            add_shares(pair - 2)
 
         return carry
 
@@ -560,7 +578,10 @@
     backward(ticks - 1, False, True)
     send_shares(ticks // 2 - 1)
     give_delta(last_hidden)
-    add_shares(ticks // 2 - 2)
+    for pair in range(max(ticks // 2 - 3, 0), ticks // 2):
+        add_shares(pair)
+    sums_out[...] = totals[1].astype(jnp.bfloat16)
+    sums_copy.start()
 
     for which in range(2):
         mate_copy(which, 0).wait_send()
@@ -590,10 +611,11 @@
 
         lax.fori_loop(1, ticks, drain, 0)
 
-    add_shares(ticks // 2 - 1)
+    sums_copy.wait()
+    summed = totals[0] + sums_in[...].astype(jnp.float32)
     factor = 1.0 / (ticks * ROWS)
-    down_out[...] = (totals[0:RANK] * (own_gain * factor)).astype(jnp.bfloat16)
-    up_out[...] = (totals[RANK : 2 * RANK] * factor).astype(jnp.bfloat16)
+    down_out[...] = (summed[0:RANK] * (own_gain * factor)).astype(jnp.bfloat16)
+    up_out[...] = (summed[RANK : 2 * RANK] * factor).astype(jnp.bfloat16)
 
     def drain_shares(pair, carry):
         all_shares(pair).wait_send()
@@ -639,7 +661,7 @@
             pltpu.VMEM((ticks + 1,) + message, bf16),
             pltpu.VMEM((ticks,) + message, bf16),
             pltpu.VMEM(shares, bf16),
-            pltpu.VMEM(shares, bf16),
+            pltpu.VMEM((ticks // 2, 2, CHIPS, 2, 2 * ROWS, LANES + 128), bf16),
             pltpu.VMEM(delta_exp.shape[2:], jnp.int32),
             pltpu.VMEM(message, bf16),
             pltpu.VMEM(message, bf16),
@@ -649,7 +671,9 @@
             pltpu.VMEM((ticks + 1, 4, ROWS, 128), f32),
             pltpu.VMEM((2,) + message, f32),
             pltpu.VMEM(message, f32),
-            pltpu.VMEM((2 * RANK, LANES), f32),
+            pltpu.VMEM((2, 2 * RANK, LANES), f32),
+            pltpu.VMEM((2 * RANK, LANES), bf16),
+            pltpu.VMEM((2 * RANK, LANES), bf16),
             pltpu.SemaphoreType.DMA((len(operands),)),
             pltpu.SemaphoreType.DMA((2, 2 * CHIPS)),
             pltpu.SemaphoreType.DMA((2, PARTS)),
@@ -659,8 +683,8 @@
             pltpu.SemaphoreType.DMA((ticks, CHUNKS)),
             pltpu.SemaphoreType.DMA((ticks // 2,)),
             pltpu.SemaphoreType.DMA((ticks // 2,)),
-            pltpu.SemaphoreType.DMA((2,)),
-            pltpu.SemaphoreType.DMA((2,)),
+            pltpu.SemaphoreType.DMA((3,)),
+            pltpu.SemaphoreType.DMA((3,)),
         ],
         compiler_params=pltpu.CompilerParams(
             collective_id=0, has_side_effects=True, vmem_limit_bytes=56 * 1024 * 1024

time: 149 us -> 131 us (0.88)
  Pallas kernels: 143 us -> 126 us
    pallas_call x1, Pallas kernels: 143 us -> 126 us  [per_device(): pl.pallas_call(functools.partial(kernel, ticks, sections), out_shape=(jax...]
where the time goes in v4:
time: 131 us
  Pallas kernels  126 us (96%)
  local copies, waits for them, and re-layouts  4.51 us (3%)
    pallas_call x1, Pallas kernels, per_device(): pl.pallas_call(functools.partial(kernel, ticks, sections), out_shape=(jax...  126 us
    unnamed x3, local copies, waits for them, and re-layouts  4.51 us

profile of v4, /device:TPU:1, one launch (start us, length us, event | category | flops | bytes accessed | tf_op | source)
XLA Modules:
  0.0 130.9 jit_solution(12030736143142625998)
XLA Ops:
  0.6 125.8 %relay.1 = (bf16[64,512]{1,0:T(8,128)(2,1)}, bf16[64,512]{1,0:T(8,128)(2,1)}, bf16[8,8192]{1,0:T(8,128)(2,1)}) custom-call(s32[33]{0:T(128)} %bitcast.23, bf16[33,8,8192]{2,1,0:T(8,128)(2,1)} %bitcast.14, bf16[8,8192]{1,0:T(8,128)(2,1)} %bitcast.15, s32[16,8,64]{2,1,0:T(8,128)} %bitcast.17, s32[15,8,64]{2,1,0:T(8,128)} %bitcast.22, f32[1,8192]{1,0:T(1,128)} %gain_hbm.1, ...), custom_call_target="tpu_custom_call" | custom-call | tf_op jit(solution)/shard_map/relay/pallas_call | solution.py:645
  126.4 1.5 %copy.14 = bf16[1,512,64]{1,2,0:T(8,128)(2,1)} copy(bf16[1,512,64]{1,2,0:T(8,128)(2,1)} %bitcast.21) | data formatting | bytes 131072
  127.9 1.5 %copy.15 = bf16[1,64,512]{2,1,0:T(8,128)(2,1)} copy(bf16[1,64,512]{2,1,0:T(8,128)(2,1)} %bitcast.20) | data formatting | bytes 131072
  129.4 1.6 %copy.16 = bf16[1,1,8,8192]{3,2,1,0:T(8,128)(2,1)} copy(bf16[1,1,8,8192]{3,2,1,0:T(8,128)(2,1)} %bitcast.16) | data formatting | bytes 262144

commit v5 on v4

--- a/solution.py
+++ b/solution.py
@@ -135,6 +135,7 @@
     backward_out,
     shares_out,
     shares_in,
+    last_in,
     exps_in,
     copy_out,
     copy_in,
@@ -458,6 +459,48 @@
             device_id={"dp": member(lax.rem(number + 1, CHIPS), side)},
         )
 
+    last_pair = ticks // 2 - 1
+
+    def first_copy(offset, other):
+        to = lax.rem(number + offset, CHIPS)
+        return pltpu.make_async_remote_copy(
+            src_ref=shares_out.at[last_pair, member(to, 1 - side if other else side), 0],
+            dst_ref=shares_in.at[last_pair, other, number, 0],
+            send_sem=share_send.at[last_pair],
+            recv_sem=share_recv.at[last_pair],
+            device_id={"dp": member(to, side)},
+        )
+
+    def all_first():
+        seven = shares_in.at[last_pair, :, pl.ds(0, CHIPS - 1), 0]
+        return pltpu.make_async_remote_copy(
+            src_ref=seven,
+            dst_ref=seven,
+            send_sem=share_send.at[last_pair],
+            recv_sem=share_recv.at[last_pair],
+            device_id={"dp": member(lax.rem(number + 1, CHIPS), side)},
+        )
+
+    def second_copy(offset):
+        to = lax.rem(me + offset, PARTS)
+        return pltpu.make_async_remote_copy(
+            src_ref=shares_out.at[last_pair, to, 1],
+            dst_ref=last_in.at[me],
+            send_sem=share_send.at[last_pair + 1],
+            recv_sem=share_recv.at[last_pair + 1],
+            device_id={"dp": to},
+        )
+
+    def all_second():
+        others = last_in.at[pl.ds(0, PARTS - 1)]
+        return pltpu.make_async_remote_copy(
+            src_ref=others,
+            dst_ref=others,
+            send_sem=share_send.at[last_pair + 1],
+            recv_sem=share_recv.at[last_pair + 1],
+            device_id={"dp": lax.rem(me + 1, PARTS)},
+        )
+
     sums_copy = pltpu.make_async_remote_copy(
         src_ref=sums_out,
         dst_ref=sums_in,
@@ -524,6 +567,30 @@
             both = shares_in[pair, other].reshape(CHIPS * 4 * ROWS, LANES + 128)
             totals[other] += dot(both[:, LANES:], both[:, :LANES], TN)
 
+    def send_first():
+        for offset in range(1, CHIPS):
+            for other in range(2):
+                first_copy(offset, other).start()
+        for other in range(2):
+            own = shares_out[last_pair, member(number, 1 - side if other else side), 0]
+            shares_in[last_pair, other, number, 0] = own
+
+    def add_first():
+        all_first().wait_recv()
+        for other in range(2):
+            both = shares_in[last_pair, other, :, 0].reshape(CHIPS * 2 * ROWS, LANES + 128)
+            totals[other] += dot(both[:, LANES:], both[:, :LANES], TN)
+
+    def send_second():
+        for offset in range(1, PARTS):
+            second_copy(offset).start()
+        last_in[me] = shares_out[last_pair, me, 1]
+
+    def add_second():
+        all_second().wait_recv()
+        both = last_in[...].reshape(PARTS * 2 * ROWS, LANES + 128)
+        totals[0] += dot(both[:, LANES:], both[:, :LANES], TN)
+
     forward(0, True, False)
 
     @pl.when(is_upper)
@@ -568,20 +635,26 @@
     def _():
         copy_copy.wait_recv()
 
+    @pl.when(is_upper)
+    def _():
+        send_first()
+
     spread_forward(ticks - 1, True)
     last_hidden = forward(ticks - 1, False, True)
 
     @pl.when(is_lower)
     def _():
         backward(ticks - 2, False, False)
+        send_first()
 
     backward(ticks - 1, False, True)
-    send_shares(ticks // 2 - 1)
-    give_delta(last_hidden)
-    for pair in range(max(ticks // 2 - 3, 0), ticks // 2):
+    send_second()
+    for pair in range(max(last_pair - 2, 0), last_pair):
         add_shares(pair)
+    add_first()
     sums_out[...] = totals[1].astype(jnp.bfloat16)
     sums_copy.start()
+    give_delta(last_hidden)
 
     for which in range(2):
         mate_copy(which, 0).wait_send()
@@ -611,6 +684,7 @@
 
         lax.fori_loop(1, ticks, drain, 0)
 
+    add_second()
     sums_copy.wait()
     summed = totals[0] + sums_in[...].astype(jnp.float32)
     factor = 1.0 / (ticks * ROWS)
@@ -621,7 +695,9 @@
         all_shares(pair).wait_send()
         return carry
 
-    lax.fori_loop(0, ticks // 2, drain_shares, 0)
+    lax.fori_loop(0, last_pair, drain_shares, 0)
+    all_first().wait_send()
+    all_second().wait_send()
 
 
 def per_device(stored_inputs, slot_ids, incoming, delta_exp, grad_exp, norm_gain, down_weight, up_weight):
@@ -662,6 +738,7 @@
             pltpu.VMEM((ticks,) + message, bf16),
             pltpu.VMEM(shares, bf16),
             pltpu.VMEM((ticks // 2, 2, CHIPS, 2, 2 * ROWS, LANES + 128), bf16),
+            pltpu.VMEM((PARTS, 2 * ROWS, LANES + 128), bf16),
             pltpu.VMEM(delta_exp.shape[2:], jnp.int32),
             pltpu.VMEM(message, bf16),
             pltpu.VMEM(message, bf16),
@@ -681,8 +758,8 @@
             pltpu.SemaphoreType.DMA((ticks, CHUNKS)),
             pltpu.SemaphoreType.DMA((ticks, CHUNKS)),
             pltpu.SemaphoreType.DMA((ticks, CHUNKS)),
-            pltpu.SemaphoreType.DMA((ticks // 2,)),
-            pltpu.SemaphoreType.DMA((ticks // 2,)),
+            pltpu.SemaphoreType.DMA((ticks // 2 + 1,)),
+            pltpu.SemaphoreType.DMA((ticks // 2 + 1,)),
             pltpu.SemaphoreType.DMA((3,)),
             pltpu.SemaphoreType.DMA((3,)),
         ],

time: 131 us -> 126 us (0.962)
  Pallas kernels: 126 us -> 121 us
    pallas_call x1, Pallas kernels: 126 us -> 121 us  [per_device(): pl.pallas_call(functools.partial(kernel, ticks, sections), out_shape=(jax...]
where the time goes in v5:
time: 126 us
  Pallas kernels  121 us (96%)
  local copies, waits for them, and re-layouts  4.51 us (4%)
    pallas_call x1, Pallas kernels, per_device(): pl.pallas_call(functools.partial(kernel, ticks, sections), out_shape=(jax...  121 us
    unnamed x3, local copies, waits for them, and re-layouts  4.51 us

profile of v5, /device:TPU:1, one launch (start us, length us, event | category | flops | bytes accessed | tf_op | source)
XLA Modules:
  0.0 126.0 jit_solution(2888285205975424711)
XLA Ops:
  0.6 120.9 %relay.1 = (bf16[64,512]{1,0:T(8,128)(2,1)}, bf16[64,512]{1,0:T(8,128)(2,1)}, bf16[8,8192]{1,0:T(8,128)(2,1)}) custom-call(s32[33]{0:T(128)} %bitcast.23, bf16[33,8,8192]{2,1,0:T(8,128)(2,1)} %bitcast.14, bf16[8,8192]{1,0:T(8,128)(2,1)} %bitcast.15, s32[16,8,64]{2,1,0:T(8,128)} %bitcast.17, s32[15,8,64]{2,1,0:T(8,128)} %bitcast.22, f32[1,8192]{1,0:T(1,128)} %gain_hbm.1, ...), custom_call_target="tpu_custom_call" | custom-call | tf_op jit(solution)/shard_map/relay/pallas_call | solution.py:721
  121.5 1.5 %copy.14 = bf16[1,512,64]{1,2,0:T(8,128)(2,1)} copy(bf16[1,512,64]{1,2,0:T(8,128)(2,1)} %bitcast.21) | data formatting | bytes 131072
  123.0 1.5 %copy.15 = bf16[1,64,512]{2,1,0:T(8,128)(2,1)} copy(bf16[1,64,512]{2,1,0:T(8,128)(2,1)} %bitcast.20) | data formatting | bytes 131072
  124.4 1.6 %copy.16 = bf16[1,1,8,8192]{3,2,1,0:T(8,128)(2,1)} copy(bf16[1,1,8,8192]{3,2,1,0:T(8,128)(2,1)} %bitcast.16) | data formatting | bytes 262144
